TPU v7x, 32 devices: a whole 2x2x4 slice. The times are simulated.
32 devices in a mesh: fsdp: 16 (over z, y, core), tp: 2 (over x).
Axes of the slice: x: 2, y: 2, z: 4, core: 2. Of those that a mesh axis runs over, the one named last changes fastest.
Arguments:
- tokens: bfloat16 [4096, 4096], P('fsdp', 'tp'), may hold values from -6 to 6
- w_feat: bfloat16 [3, 4096, 4096], P(None, 'fsdp', 'tp'), may hold values from -0.09375 to 0.09375
- short_filter: float32 [3, 256, 7], P(None, 'tp'), may hold values from -6 to 6
- long_filter: bfloat16 [256, 128], P('tp'), may hold values from -1.5 to 1.5
- doc_ids: int32 [4096], P('fsdp'), may hold values from 0 to 7, never falling along the last dimension, each value on 1 to 2048 neighbouring positions
- grad_out: bfloat16 [4096, 4096], P('fsdp', 'tp'), may hold values from -6 to 6
Outputs:
- mixed: bfloat16 [4096, 4096], P('fsdp', 'tp')
- input_grad: bfloat16 [4096, 4096], P('fsdp', 'tp')
Inputs may be any that keep to these rules, and one draw needn't show every extreme that they name: `doc_ids`: document numbers never fall along the positions; each document covers 1 to 2048 consecutive positions and one covers exactly 2048; every number from 0 to 7 occurs.
All inputs are finite; a program needn't handle non-finite values.
Results may differ from a plain program's by a relative error of at most 0.0081.
Values may be sent and summed in bfloat16 or wider, within the bound.
A program may use at most 192 MiB of HBM per device.

v0:
```python
import jax
import jax.numpy as jnp
from jax import lax
from jax.sharding import PartitionSpec as P


def shifted_2(value, axis, steps):
    count = lax.axis_size(axis)
    initial, last = (max(0, -steps), min(count, count - steps))
    return lax.ppermute(value, axis, [(source, source + steps) for source in range(initial, last)])


def causal_taps(extended, doc_ext, filters, lead_rows):
    row_count = extended.shape[0] - lead_rows
    doc_now = doc_ext[lead_rows:]
    bcast_shape = (row_count,) + (1,) * (extended.ndim - 1)
    summed = jnp.zeros((row_count,) + extended.shape[1:], jnp.float32)
    for offset in range(filters.shape[-1]):
        shifted = extended[lead_rows - offset : lead_rows - offset + row_count].astype(jnp.float32)
        same_doc = (
            (doc_ext[lead_rows - offset : lead_rows - offset + row_count] == doc_now)
            .astype(jnp.float32)
            .reshape(bcast_shape)
        )
        summed = summed + filters[..., offset] * shifted * same_doc
    return summed


def ahead_taps(extended, doc_ext, filters, row_count):
    doc_now = doc_ext[:row_count]
    bcast_shape = (row_count,) + (1,) * (extended.ndim - 1)
    summed = jnp.zeros((row_count,) + extended.shape[1:], jnp.float32)
    for offset in range(filters.shape[-1]):
        shifted = extended[offset : offset + row_count].astype(jnp.float32)
        same_doc = (
            (doc_ext[offset : offset + row_count] == doc_now)
            .astype(jnp.float32)
            .reshape(bcast_shape)
        )
        summed = summed + filters[..., offset] * shifted * same_doc
    return summed


def toeplitz_base(long_filter, anti_causal):
    tap_count = long_filter.shape[1]
    row_iota = lax.broadcasted_iota(jnp.int32, (tap_count, 2 * tap_count), 0)
    col_iota = lax.broadcasted_iota(jnp.int32, (tap_count, 2 * tap_count), 1)
    if anti_causal:
        lag_index = col_iota - row_iota
    else:
        lag_index = row_iota + tap_count - col_iota
    tap_iota = lax.broadcasted_iota(jnp.int32, (tap_count, tap_count, 2 * tap_count), 0)
    one_hot = (
        (tap_iota == lag_index[None])
        .astype(long_filter.dtype)
        .reshape(tap_count, 2 * tap_count * tap_count)
    )
    table = jnp.dot(long_filter, one_hot, preferred_element_type=jnp.float32).astype(
        long_filter.dtype
    )
    return table.reshape(long_filter.shape[0], tap_count, 2 * tap_count)


def blocked_conv(extended, doc_ext, toeplitz, doc_rows, row_count):
    groups = toeplitz.shape[0]
    tap_count = toeplitz.shape[1]
    chan_width = extended.shape[1]
    block_count = row_count // tap_count
    row_blocks = extended.reshape(block_count + 1, tap_count, chan_width)
    windows = jnp.concatenate([row_blocks[:-1], row_blocks[1:]], axis=1)
    doc_blocks = doc_ext.reshape(block_count + 1, tap_count)
    doc_windows = jnp.concatenate([doc_blocks[:-1], doc_blocks[1:]], axis=1)
    row_docs = doc_rows.reshape(block_count, tap_count)

    def one_block(inputs):
        window, col_docs, own_docs = inputs
        window = window.reshape(2 * tap_count, groups, chan_width // groups)
        kernel = toeplitz * (own_docs[:, None] == col_docs[None, :]).astype(toeplitz.dtype)[None]
        result = jnp.einsum("gtu,ugk->tgk", kernel, window, preferred_element_type=jnp.float32)
        return result.reshape(tap_count, chan_width)

    blocks = lax.map(one_block, (windows, doc_windows, row_docs))
    return blocks.reshape(row_count, chan_width)


def shards(tokens, w_feat, short_filter, long_filter, doc_ids, grad_out):
    rows_here = tokens.shape[0]
    tap_count = long_filter.shape[1]
    margin = 8
    reach_rows = tap_count + margin
    gathered = lax.all_gather(tokens, "tp", axis=1, tiled=True)
    filter_groups = short_filter.shape[1]
    short_full = jnp.broadcast_to(
        short_filter[:, :, None, :], (3, filter_groups, 16, short_filter.shape[2])
    ).reshape(3, filter_groups * 16, short_filter.shape[2])
    w_whole = lax.all_gather(w_feat, "fsdp", axis=1, tiled=True)
    u_all = jnp.einsum("sd,jdc->sjc", gathered, w_whole, preferred_element_type=jnp.float32).astype(
        jnp.bfloat16
    )
    u_pair = u_all[:, 1:]
    prev_pair, prev_doc = shifted_2(
        (u_pair[rows_here - reach_rows :], doc_ids[rows_here - reach_rows :]), "fsdp", 1
    )
    ext_pair = jnp.concatenate([prev_pair, u_pair], axis=0)
    ext_doc = jnp.concatenate([prev_doc, doc_ids], axis=0)
    conv_pair = causal_taps(ext_pair, ext_doc, short_full[1:], margin)
    product_kv = (conv_pair[:, 0] * conv_pair[:, 1]).astype(jnp.bfloat16)
    doc_product = ext_doc[margin:]
    long_out = blocked_conv(
        product_kv, doc_product, toeplitz_base(long_filter, False), doc_ids, rows_here
    )
    conv_pair, long_out, prev_doc = (
        conv_pair[tap_count:],
        long_out,
        prev_doc[reach_rows - margin :],
    )
    u_query = u_all[:, 0]
    prev_query = shifted_2(u_query[rows_here - margin :], "fsdp", 1)
    ext_query = jnp.concatenate([prev_query, u_query], axis=0)
    ext_doc = jnp.concatenate([prev_doc, doc_ids], axis=0)
    conv_query = causal_taps(ext_query, ext_doc, short_full[0], margin)
    pieces = ((0, 3, w_whole),)
    block_out = (conv_query * long_out).astype(jnp.bfloat16)
    grad_float = grad_out.astype(jnp.float32)
    grad_long = (grad_float * conv_query).astype(jnp.bfloat16)
    grad_query = grad_float * long_out
    next_grad, next_doc = shifted_2((grad_long[:tap_count], doc_ids[:tap_count]), "fsdp", -1)
    ext_grad = jnp.concatenate([grad_long, next_grad], axis=0)
    ext_doc = jnp.concatenate([doc_ids, next_doc], axis=0)
    grad_mixed = blocked_conv(
        ext_grad, ext_doc, toeplitz_base(long_filter, True), doc_ids, rows_here
    )
    grad_feat = jnp.stack(
        [grad_query, grad_mixed * conv_pair[:, 1], grad_mixed * conv_pair[:, 0]], axis=1
    ).astype(jnp.bfloat16)
    next_feat = shifted_2(grad_feat[:margin], "fsdp", -1)
    ext_feat = jnp.concatenate([grad_feat, next_feat], axis=0)
    doc_feat = jnp.concatenate([doc_ids, next_doc[:margin]], axis=0)
    grad_u = ahead_taps(ext_feat, doc_feat, short_full, rows_here).astype(jnp.bfloat16)
    first_role, end_role, weights = pieces[0]
    partial_value = jnp.einsum("sjc,jdc->sd", grad_u, weights, preferred_element_type=jnp.float32)
    input_grad = lax.psum_scatter(
        partial_value.astype(jnp.bfloat16), "tp", scatter_dimension=1, tiled=True
    )
    return (block_out, input_grad)


def solution(mesh):
    in_specs = (
        P("fsdp", "tp"),
        P(None, "fsdp", "tp"),
        P(None, "tp", None),
        P("tp", None),
        P("fsdp"),
        P("fsdp", "tp"),
    )
    out_specs = (P("fsdp", "tp"), P("fsdp", "tp"))
    return jax.shard_map(shards, mesh=mesh, in_specs=in_specs, out_specs=out_specs, check_vma=False)
```

profile of v0, /device:TPU:0, one launch (start us, length us, event | category | flops | bytes accessed | tf_op | source)
XLA Modules:
  0.0 490.7 jit_solution(5397390255139693855)
XLA Ops:
  7.3 0.7 all-gather.3.cloned.1.call-update
  8.0 0.7 all-gather.5.cloned.1.call-update
  8.8 2.3 collective-permute-start.1
  11.2 1.3 collective-permute-start.4
  12.5 0.2 broadcast_in_dim.27
  12.7 0.3 broadcast_in_dim.28
  13.2 0.3 broadcast_in_dim.29
  13.5 0.5 slice.329
  13.9 0.4 broadcast_in_dim.30
  14.4 0.8 reshape.228
  15.2 0.1 fusion.59
  15.4 0.2 iota.51
  15.6 4.7 convolution_convert_fusion
  20.4 4.6 convolution_convert_fusion.1
  25.0 12.7 %copy.35 = bf16[128,128,256]{2,1,0:T(8,128)(2,1)} copy(bf16[128,128,256]{0,2,1:T(8,128)(2,1)} %bitcast.135) | data formatting | bytes 16777216 | tf_op jit(solution)/shard_map/while | solution.py:82
  37.7 12.7 %copy.31 = bf16[128,128,256]{2,1,0:T(8,128)(2,1)} copy(bf16[128,128,256]{0,2,1:T(8,128)(2,1)} %bitcast.136) | data formatting | bytes 16777216 | tf_op jit(solution)/shard_map/while | solution.py:82
  50.7 243.4 %all-gather.5.cloned.1.call-done = bf16[3,4096,2048]{2,1,0:T(8,128)(2,1)} async-done(((bf16[3,256,2048]{2,1,0:T(8,128)(2,1)}), bf16[3,4096,2048]{2,1,0:T(8,128)(2,1)}) %all-gather.5.cloned.1.call-update) | async-done | bytes 50331664 | tf_op jit(solution)/shard_map/all_gather | solution.py:96
  294.1 21.2 %convolution_convert_fusion.2 = bf16[256,3,2048]{2,0,1:T(8,128)(2,1)S(1)} fusion(bf16[3,4096,2048]{2,1,0:T(8,128)(2,1)} %all-gather.5.cloned.1.call-done, bf16[256,4096]{1,0:T(8,128)(2,1)} %all-gather.3.cloned.1.call-done), kind=kOutput, calls=%fused_computation.42 | convolution fusion | flops 12886474752 | bytes 55574528 | tf_op jit(solution)/shard_map/sd,jdc->sjc/dot_general | solution.py:97
  315.4 2.2 collective-permute-start
  317.6 0.7 collective-permute-done
  318.4 4.0 fusion.42
  322.4 1.5 collective-permute-start.3
  324.0 1.1 slice.412
  325.1 1.5 slice.413
  326.6 4.5 collective-permute-start.2
  331.1 0.7 copy.33
  331.7 1.1 pad_maximum_fusion.5
  332.9 0.7 copy.34
  333.5 1.6 pad_maximum_fusion.4
  335.1 1.6 broadcast.89.clone2.1
  336.7 17.0 %while.21 = (s32[]{:T(128)}, f32[2,128,2048]{2,1,0:T(8,128)}, bf16[2,256,2048]{1,2,0:T(8,128)(2,1)}, s32[2,128]{1,0:T(2,128)S(1)}, s32[2,256]{1,0:T(2,128)S(1)}, /*index=5*/bf16[128,128,256]{2,1,0:T(8,128)(2,1)}, s32[]{:T(128)}) while((s32[]{:T(128)}, f32[2,128,2048]{2,1,0:T(8,128)}, bf16[2,256,2048]{1,2,0:T(8,128)(2,1)}, ...), condition=%wide.region_3.4_spmd, body=%wide.region_2.3_spmd.sunk | while | flops 138477568 | bytes 16913496 | solution.py:82
  336.8 1.3 constant_dynamic-slice_fusion.12
  338.1 5.7 %fusion.83 = f32[128,16,128]{2,1,0:T(8,128)S(1)} fusion(bf16[256,128,16]{0,2,1:T(8,128)(2,1)S(1)} %bitcast.131, bf16[128,128,256]{2,1,0:T(8,128)(2,1)} %get-tuple-element.307, bf16[128,256]{1,0:T(8,128)(2,1)S(1)} %compare_convert_fusion.17), kind=kOutput, calls=%fused_computation.9.clone.1 | convolution fusion | flops 138412032 | bytes 10551296 | tf_op jit(solution)/shard_map/while/body/eval_jaxpr/gtu,ugk->tgk/dot_general | solution.py:79
  343.8 0.3 copy.61
  344.2 1.1 constant_dynamic-update-slice_fusion.5
  345.3 1.3 constant_dynamic-slice_fusion.12
  346.6 5.7 %fusion.83 = f32[128,16,128]{2,1,0:T(8,128)S(1)} fusion(bf16[256,128,16]{0,2,1:T(8,128)(2,1)S(1)} %bitcast.131, bf16[128,128,256]{2,1,0:T(8,128)(2,1)} %get-tuple-element.307, bf16[128,256]{1,0:T(8,128)(2,1)S(1)} %compare_convert_fusion.17), kind=kOutput, calls=%fused_computation.9.clone.1 | convolution fusion | flops 138412032 | bytes 10551296 | tf_op jit(solution)/shard_map/while/body/eval_jaxpr/gtu,ugk->tgk/dot_general | solution.py:79
  352.3 0.3 copy.61
  352.7 1.1 constant_dynamic-update-slice_fusion.5
  353.8 20.9 %multiply_add_fusion = f32[384,2,2048]{2,0,1:T(8,128)S(1)} fusion(bf16[256,2,2048]{2,0,1:T(8,128)(2,1)} %slice.413, bf16[136,2,2048]{2,0,1:T(8,128)(2,1)} %collective-permute-done.2, f32[384]{0:T(512)S(1)} %get-tuple-element.172, f32[2,2048]{1,0:T(2,128)S(1)} %get-tuple-element.146, f32[384]{0:T(512)S(1)} %get-tuple-element.173, ...), kind=kLoop, calls=%fused_computation.33 | loop fusion | flops 73924608 | bytes 9626624 | tf_op jit(solution)/shard_map/add | solution.py:25
  374.7 0.4 fusion.27
  375.1 1.2 copy-done.3
  376.3 1.7 fusion.44
  378.0 1.2 fusion.58
  379.2 1.6 copy.29
  380.8 1.3 copy.30
  382.1 2.8 pad_maximum_fusion.3
  385.0 1.6 broadcast.89.clone2
  386.5 17.0 %while.20 = (s32[]{:T(128)}, f32[2,128,2048]{2,1,0:T(8,128)}, bf16[2,256,2048]{1,2,0:T(8,128)(2,1)}, s32[2,128]{1,0:T(2,128)S(1)}, s32[2,256]{1,0:T(2,128)S(1)}, /*index=5*/bf16[128,128,256]{2,1,0:T(8,128)(2,1)}, s32[]{:T(128)}) while((s32[]{:T(128)}, f32[2,128,2048]{2,1,0:T(8,128)}, bf16[2,256,2048]{1,2,0:T(8,128)(2,1)}, ...), condition=%wide.region_1.2_spmd, body=%wide.region_0.1_spmd.sunk | while | flops 138477568 | bytes 16913496 | solution.py:82
  386.6 1.3 constant_dynamic-slice_fusion.10
  388.0 5.7 %fusion.79 = f32[128,16,128]{2,1,0:T(8,128)S(1)} fusion(bf16[256,128,16]{0,2,1:T(8,128)(2,1)S(1)} %bitcast.132, bf16[128,128,256]{2,1,0:T(8,128)(2,1)} %get-tuple-element.286, bf16[128,256]{1,0:T(8,128)(2,1)S(1)} %compare_convert_fusion.16), kind=kOutput, calls=%fused_computation.clone.1 | convolution fusion | flops 138412032 | bytes 10551296 | tf_op jit(solution)/shard_map/while/body/eval_jaxpr/gtu,ugk->tgk/dot_general | solution.py:79
  393.6 0.3 copy.60
  394.0 1.0 constant_dynamic-update-slice_fusion.4
  395.1 1.3 constant_dynamic-slice_fusion.10
  396.4 5.7 %fusion.79 = f32[128,16,128]{2,1,0:T(8,128)S(1)} fusion(bf16[256,128,16]{0,2,1:T(8,128)(2,1)S(1)} %bitcast.132, bf16[128,128,256]{2,1,0:T(8,128)(2,1)} %get-tuple-element.286, bf16[128,256]{1,0:T(8,128)(2,1)S(1)} %compare_convert_fusion.16), kind=kOutput, calls=%fused_computation.clone.1 | convolution fusion | flops 138412032 | bytes 10551296 | tf_op jit(solution)/shard_map/while/body/eval_jaxpr/gtu,ugk->tgk/dot_general | solution.py:79
  402.1 0.3 copy.60
  402.4 1.1 constant_dynamic-update-slice_fusion.4
  403.5 4.2 fusion.41
  407.7 0.3 pad_maximum_fusion.2
  408.0 1.3 collective-permute-start.5
  409.4 4.1 collective-permute-done.5
  413.5 1.9 pad_maximum_fusion
  415.4 31.4 %fusion.14 = bf16[256,4096]{1,0:T(8,128)(2,1)} fusion(bf16[3,4096,2048]{2,1,0:T(8,128)(2,1)} %all-gather.5.cloned.1.call-done, bf16[264,3,2048]{2,0,1:T(8,128)(2,1)} %pad_maximum_fusion, f32[256]{0:T(256)S(1)} %get-tuple-element.163, f32[3,2048]{1,0:T(4,128)S(1)} %get-tuple-element.187, f32[256]{0:T(256)S(1)} %get-tuple-element.164, ...), kind=kOutput, calls=%fused_computation.35 | convolution fusion | flops 12931563520 | bytes 74627072 | tf_op jit(solution)/shard_map/sjc,jdc->sd/dot_general | solution.py:141
  446.8 37.3 %reduce-scatter.2.cloned.1.call-done = bf16[256,2048]{1,0:T(8,128)(2,1)} async-done(((bf16[256,4096]{1,0:T(8,128)(2,1)}), bf16[256,2048]{1,0:T(8,128)(2,1)}) %reduce-scatter.2.cloned.1.call-update) | async-done | bytes 1048592 | tf_op jit(solution)/shard_map/reduce_scatter | solution.py:142
  (65 shorter events, 1.6 us)
Async XLA Ops:
  7.2 8.5 %copy-start = (bf16[128,128]{1,0:T(8,128)(2,1)S(1)}, bf16[128,128]{1,0:T(8,128)(2,1)}, u32[]{:S(2)}) copy-start(bf16[128,128]{1,0:T(8,128)(2,1)} %param.13) | copy-start | bytes 98308
  7.2 1.6 copy-start.6
  7.2 5.3 %copy-start.5 = (f32[3,128,7]{1,2,0:T(8,128)S(1)}, f32[3,128,7]{1,2,0:T(8,128)}, u32[]{:S(2)}) copy-start(f32[3,128,7]{1,2,0:T(8,128)} %param.12) | copy-start | bytes 32260
  7.2 5.9 %slice-start = ((f32[3,128,7]{1,2,0:T(8,128)}), f32[2,128,7]{1,2,0:T(8,128)S(1)}, s32[]{:S(2)}) async-start(f32[3,128,7]{1,2,0:T(8,128)} %param.12), calls=%async_computation.4 | async-start | bytes 16384 | tf_op jit(solution)/shard_map/slice | solution.py:106
  7.2 43.5 %all-gather.3.cloned.1.call-start = ((), (), s32[]{:S(2)}) async-start(), calls=%async_computation.1 | async-start | bytes 3145728 | tf_op jit(solution)/shard_map/all_gather | solution.py:91
  7.9 286.2 %all-gather.5.cloned.1.call-start = ((), (), s32[]{:S(2)}) async-start(), calls=%async_computation.2 | async-start | bytes 53477376 | tf_op jit(solution)/shard_map/all_gather | solution.py:96
  8.7 475.5 %reduce-scatter.2.cloned.1.call-start = ((), (), s32[]{:S(2)}) async-start(), calls=%async_computation.3 | async-start | bytes 3145728 | tf_op jit(solution)/shard_map/reduce_scatter | solution.py:142
  8.8 41.5 %collective-permute-start.1 = (s32[136]{0:T(256)S(1)}, s32[136]{0:T(256)S(1)}, u32[]{:S(2)}, u32[]{:S(2)}) collective-permute-start(s32[136]{0:T(256)S(1)} %slice.310), channel_id=1, source_target_pairs={{0,2},{2,4},{4,6},{6,8},{8,10},{10,12},{12,14},{14,16},{16,18},{18... | collective-permute-start | bytes 1640 | tf_op jit(solution)/shard_map/ppermute | solution.py:10
  11.2 39.2 %collective-permute-start.4 = (s32[128]{0:T(128)S(1)}, s32[128]{0:T(128)S(1)}, u32[]{:S(2)}, u32[]{:S(2)}) collective-permute-start(s32[128]{0:T(128)S(1)} %slice.367), channel_id=1, source_target_pairs={{2,0},{4,2},{6,4},{8,6},{10,8},{12,10},{14,12},{16,14},{18,16},{20... | collective-permute-start | bytes 1544 | tf_op jit(solution)/shard_map/ppermute | solution.py:10
  50.6 267.7 %copy-start.4 = (bf16[256,2048]{1,0:T(8,128)(2,1)S(1)}, bf16[256,2048]{1,0:T(8,128)(2,1)}, u32[]{:S(2)}) copy-start(bf16[256,2048]{1,0:T(8,128)(2,1)} %param.15) | copy-start | bytes 3145732
  315.4 3.0 collective-permute-start
  322.4 9.4 %collective-permute-start.3 = (bf16[128,2048]{1,0:T(8,128)(2,1)S(1)}, bf16[128,2048]{1,0:T(8,128)(2,1)}, u32[]{:S(2)}, u32[]{:S(2)}) collective-permute-start(bf16[128,2048]{1,0:T(8,128)(2,1)S(1)} %slice.437), channel_id=1, source_target_pairs={{2,0},{4,2},{6,4},{8,6},{10,8},{12,10},{14,12},{16,14},{18,16},{20... | collective-permute-start | bytes 1572872 | tf_op jit(solution)/shard_map/ppermute | solution.py:10
  326.6 27.2 %collective-permute-start.2 = (bf16[136,2,2048]{2,0,1:T(8,128)(2,1)}, bf16[136,2,2048]{2,0,1:T(8,128)(2,1)}, u32[]{:S(2)}, u32[]{:S(2)}) collective-permute-start(bf16[136,2,2048]{2,0,1:T(8,128)(2,1)} %slice.412), channel_id=1, source_target_pairs={{0,2},{2,4},{4,6},{6,8},{8,10},{10,12},{12,14},{14,16},{16,18},{18... | collective-permute-start | bytes 3342344 | tf_op jit(solution)/shard_map/ppermute | solution.py:10
  374.7 1.6 copy-start.3
  403.5 4.2 copy-start.2
  408.0 5.5 %collective-permute-start.5 = (bf16[8,3,2048]{2,0,1:T(8,128)(2,1)S(1)}, bf16[8,3,2048]{2,0,1:T(8,128)(2,1)S(1)}, u32[]{:S(2)}, u32[]{:S(2)}) collective-permute-start(bf16[8,3,2048]{2,0,1:T(8,128)(2,1)S(1)} %slice.441), channel_id=1, source_target_pairs={{2,0},{4,2},{6,4},{8,6},{10,8},{12,10},{14,12},{16,14},{18,16},{20... | collective-permute-start | bytes 294920 | tf_op jit(solution)/shard_map/ppermute | solution.py:10
  415.4 68.7 %copy-start.1 = (bf16[128,128]{1,0:T(8,128)(2,1)S(1)}, bf16[128,128]{1,0:T(8,128)(2,1)}, u32[]{:S(2)}) copy-start(bf16[128,128]{1,0:T(8,128)(2,1)} %param.13) | copy-start | bytes 98308
Sparse Core Ops, SparseCore 0:
  9.6 35.8 all-gather.2
  47.0 247.0 all-gather.4
  446.9 37.1 reduce-scatter.1
where the time goes:
time: 492 us; the launch traced here: 491 us
  waiting for transfers between devices  287 us (58%)
  matrix products  84.6 us (17%)
  local copies, waits for them, and re-layouts  52.1 us (11%)
  other arithmetic  39.6 us (8%)
  between operations  14.1 us (3%)
  starting transfers between devices  13.2 us (3%)
    all_gather x1, waiting for transfers between devices, shards(): w_whole = lax.all_gather(w_feat, 'fsdp', axis=1, tiled=True)  243 us
    reduce_scatter x1, waiting for transfers between devices, shards(): lax.psum_scatter(partial_value.astype(jnp.bfloat16), 'tp', scatter_dimens...  37.3 us
    dot_general x1, matrix products, shards(): jnp.einsum('sjc,jdc->sd', grad_u, weights, preferred_element_type=jnp.flo...  31.4 us
    while x2, local copies, waits for them, and re-layouts, blocked_conv(): blocks = lax.map(one_block, (windows, doc_windows, row_docs))  25.4 us
    dot_general x4, matrix products, one_block(): jnp.einsum('gtu,ugk->tgk', kernel, window, preferred_element_type=jnp.flo...  22.6 us
    dot_general x1, matrix products, shards(): jnp.einsum('sd,jdc->sjc', gathered, w_whole, preferred_element_type=jnp.f...  21.2 us
    add x1, other arithmetic, causal_taps(): summed = summed + filters[..., offset] * shifted * same_doc  20.9 us
    ppermute x6, starting transfers between devices, shifted_2(): lax.ppermute(value, axis, [(source, source + steps) for source in range(i...  13.1 us
  transfers between devices with their start and end apart: 9, of which 4 were waited for; matrix products, arithmetic and copies ran while one was open for 13% of the time, Pallas kernels for 0%

commit v1 on v0

v1 whole, which is shorter than its diff:
```python
import functools

import jax
import jax.numpy as jnp
from jax import lax
from jax.experimental import pallas as pl
from jax.experimental.pallas import tpu as pltpu
from jax.sharding import PartitionSpec as P

LANES = 128
EDGE = 16


def shifted(value, axis, steps):
    count = lax.axis_size(axis)
    first, last = max(0, -steps), min(count, count - steps)
    return lax.ppermute(value, axis, [(at, at + steps) for at in range(first, last)])


def rotated(value, axis, steps):
    count = lax.axis_size(axis)
    return lax.ppermute(value, axis, [(at, (at + steps) % count) for at in range(count)])


def gather_columns(value, axis):
    count = lax.axis_size(axis)
    width = value.shape[1]
    here = lax.axis_index(axis)
    whole = jnp.zeros((value.shape[0], width * count), value.dtype)
    for step in range(count):
        block = value if step == 0 else rotated(value, axis, step)
        owner = (here - step) % count
        whole = lax.dynamic_update_slice(whole, block, (0, owner * width))
    return whole


def toeplitz(long_filter, anti_causal):
    taps = long_filter.shape[1]
    row = lax.broadcasted_iota(jnp.int32, (taps, 2 * taps), 0)
    column = lax.broadcasted_iota(jnp.int32, (taps, 2 * taps), 1)
    lag = column - row if anti_causal else row + taps - column
    tap = lax.broadcasted_iota(jnp.int32, (taps, taps, 2 * taps), 0)
    one_hot = (tap == lag[None]).astype(long_filter.dtype).reshape(taps, 2 * taps * taps)
    table = jnp.dot(long_filter, one_hot, preferred_element_type=jnp.float32)
    return table.astype(long_filter.dtype).reshape(long_filter.shape[0], taps, 2 * taps)


def conv_kernel(
    rows, taps, short,
    u_q, u_kv, grad, filters, t_fwd, t_bwd, m_fwd, m_bwd, back, ahead,
    mixed, grad_u,
    f32_u, conv, prod, glong, feat,
):
    near = rows + EDGE
    far = rows + taps + EDGE
    groups = t_fwd.shape[0]
    lane_group = lax.broadcasted_iota(jnp.int32, (1, LANES), 1) // (LANES // groups)

    def short_conv(role, source, first):
        f32_u[...] = source.astype(jnp.float32)
        total = filters[role, 0:1, :] * f32_u[pl.ds(EDGE, far), :]
        for i in range(1, short):
            term = filters[role, i : i + 1, :] * f32_u[pl.ds(EDGE - i, far), :]
            total = total + jnp.where(back[pl.ds(first, far), :] >= i, term, 0.0)
        return total

    conv[0] = short_conv(0, u_q[...], taps)
    conv[1] = short_conv(1, u_kv[0], 0)
    conv[2] = short_conv(2, u_kv[1], 0)
    pad = jnp.zeros((prod.shape[0] - far, LANES), prod.dtype)
    prod[pl.ds(0, far), :] = (conv[1] * conv[2]).astype(prod.dtype)
    prod[pl.ds(far, pad.shape[0]), :] = pad
    glong[pl.ds(0, far), :] = (grad[...].astype(jnp.float32) * conv[0]).astype(glong.dtype)
    glong[pl.ds(far, pad.shape[0]), :] = pad

    def long_conv(table, masks, source, start):
        count = min(taps, near - start)
        kernel = table[:, pl.ds(0, count), :] * masks[pl.ds(start, count), :][None]
        out = jnp.dot(
            kernel.reshape(groups * count, 2 * taps),
            source[pl.ds(start, 2 * taps), :],
            preferred_element_type=jnp.float32,
        ).reshape(groups, count, LANES)
        total = jnp.where(lane_group == 0, out[0], 0.0)
        for g in range(1, groups):
            total = jnp.where(lane_group == g, out[g], total)
        return total

    def rounded(value):
        return value.astype(jnp.bfloat16).astype(jnp.float32)

    for start in range(0, near, taps):
        count = min(taps, near - start)
        here = pl.ds(start, count)
        behind = pl.ds(start + taps, count)
        lc = long_conv(t_fwd, m_fwd, prod, start)
        gm = long_conv(t_bwd, m_bwd, glong, start)
        if start < rows:
            mixed[here, :] = (conv[0, here, :] * lc).astype(mixed.dtype)
        feat[0, here, :] = rounded(grad[here, :].astype(jnp.float32) * lc)
        feat[1, here, :] = rounded(gm * conv[2, behind, :])
        feat[2, here, :] = rounded(gm * conv[1, behind, :])
    for role in range(3):
        total = filters[role, 0:1, :] * feat[role, pl.ds(0, rows), :]
        for i in range(1, short):
            term = filters[role, i : i + 1, :] * feat[role, pl.ds(i, rows), :]
            total = total + jnp.where(ahead[...] >= i, term, 0.0)
        grad_u[role] = total.astype(grad_u.dtype)


def convolve(rows, taps, short, first, u_q, u_kv, grad, filters, t_fwd, t_bwd, m_fwd, m_bwd, back, ahead):
    width = u_q.shape[1]
    wide = u_q.shape[0]
    near, far = rows + EDGE, rows + taps + EDGE
    groups = t_fwd.shape[0] * LANES // grad.shape[1]
    first = first // LANES
    padded = rows + 2 * taps
    whole = lambda *shape: pl.BlockSpec(shape, lambda n: (0,) * len(shape))
    return pl.pallas_call(
        functools.partial(conv_kernel, rows, taps, short),
        grid=(width // LANES,),
        in_specs=[
            pl.BlockSpec((wide, LANES), lambda n: (0, n)),
            pl.BlockSpec((2, wide, LANES), lambda n: (0, 0, n)),
            pl.BlockSpec((far, LANES), lambda n: (0, n + first)),
            pl.BlockSpec((3, 8, LANES), lambda n: (0, 0, n + first)),
            pl.BlockSpec((groups, taps, 2 * taps), lambda n: (n + first, 0, 0)),
            pl.BlockSpec((groups, taps, 2 * taps), lambda n: (n + first, 0, 0)),
            whole(near, 2 * taps),
            whole(near, 2 * taps),
            whole(*back.shape),
            whole(*ahead.shape),
        ],
        out_specs=[
            pl.BlockSpec((rows, LANES), lambda n: (0, n)),
            pl.BlockSpec((3, rows, LANES), lambda n: (0, 0, n)),
        ],
        out_shape=[
            jax.ShapeDtypeStruct((rows, width), jnp.bfloat16),
            jax.ShapeDtypeStruct((3, rows, width), jnp.bfloat16),
        ],
        scratch_shapes=[
            pltpu.VMEM((wide, LANES), jnp.float32),
            pltpu.VMEM((3, far, LANES), jnp.float32),
            pltpu.VMEM((padded, LANES), jnp.bfloat16),
            pltpu.VMEM((padded, LANES), jnp.bfloat16),
            pltpu.VMEM((3, near, LANES), jnp.float32),
        ],
        compiler_params=pltpu.CompilerParams(vmem_limit_bytes=24 * 1024 * 1024),
        cost_estimate=pl.CostEstimate(
            flops=width * rows * taps * 64, bytes_accessed=width * rows * 40, transcendentals=0
        ),
    )(u_q, u_kv, grad, filters, t_fwd, t_bwd, m_fwd, m_bwd, back, ahead)


def chunk_sizes(width):
    units = width // LANES
    sizes = []
    left = units
    while left > 0:
        size = max(1, min(units // 4, (left + 1) // 2))
        sizes.append(size * LANES)
        left -= size
    return sizes


def shards(tokens, w_feat, short_filter, long_filter, doc_ids, grad_out):
    rows = tokens.shape[0]
    taps = long_filter.shape[1]
    short = short_filter.shape[2]
    channels = w_feat.shape[2]
    group = channels // long_filter.shape[0]
    tp = lax.axis_size("tp")
    reach = taps + EDGE

    sizes = chunk_sizes(channels)
    weights, start = [], 0
    for size in sizes:
        part = w_feat[:, :, start : start + size]
        weights.append(lax.all_gather(part, "fsdp", axis=1, tiled=True))
        start += size

    def extended(value):
        before = shifted(value[rows - reach :], "fsdp", 1)
        after = shifted(value[:reach], "fsdp", -1)
        return jnp.concatenate([before, value, after], axis=0)

    tokens_ext = gather_columns(extended(tokens), "tp")
    docs = extended(doc_ids + 1) - 1
    grad_ext = jnp.concatenate([grad_out, shifted(grad_out[:reach], "fsdp", -1)], axis=0)

    span = rows + 2 * taps + EDGE
    now = docs[EDGE : EDGE + span]
    back = sum((docs[EDGE - i : EDGE - i + span] == now).astype(jnp.int32) for i in range(1, short))
    back = jnp.broadcast_to(back[:, None], (span, LANES))
    ahead = sum(
        (docs[reach + i : reach + i + rows] == doc_ids).astype(jnp.int32) for i in range(1, short)
    )
    ahead = jnp.broadcast_to(ahead[:, None], (rows, LANES))

    near = rows + EDGE
    docs_pad = jnp.concatenate([docs, jnp.full((taps,), -1, docs.dtype)])

    def window_masks(lead):
        parts = []
        for at in range(0, near, taps):
            count = min(taps, near - at)
            own = docs_pad[reach + at : reach + at + count]
            cols = docs_pad[reach + at - lead : reach + at - lead + 2 * taps]
            parts.append(own[:, None] == cols[None, :])
        return jnp.concatenate(parts, axis=0).astype(jnp.bfloat16)

    m_fwd, m_bwd = window_masks(taps), window_masks(0)
    t_fwd, t_bwd = toeplitz(long_filter, False), toeplitz(long_filter, True)
    filters = jnp.pad(
        jnp.repeat(jnp.swapaxes(short_filter, 1, 2), group, axis=2), ((0, 0), (0, 8 - short), (0, 0))
    )

    wide = rows + taps + 2 * EDGE
    tokens_kv = tokens_ext[:wide]
    tokens_q = tokens_ext[taps:]
    mixed, partial, start = [], None, 0
    for size, w in zip(sizes, weights):
        u_q = jnp.dot(tokens_q, w[0], preferred_element_type=jnp.float32).astype(jnp.bfloat16)
        u_kv = jnp.einsum(
            "sd,jdc->jsc", tokens_kv, w[1:], preferred_element_type=jnp.float32
        ).astype(jnp.bfloat16)
        part, grad_u = convolve(
            rows, taps, short, start, u_q, u_kv, grad_ext, filters, t_fwd, t_bwd, m_fwd, m_bwd, back, ahead
        )
        mixed.append(part)
        term = jnp.einsum("jsc,jdc->sd", grad_u, w, preferred_element_type=jnp.float32)
        partial = term if partial is None else partial + term
        start += size
    mixed = jnp.concatenate(mixed, axis=1)

    partial = partial.astype(jnp.bfloat16)
    width = tokens.shape[1]
    here = lax.axis_index("tp")
    total = lax.dynamic_slice(partial, (0, here * width), (rows, width)).astype(jnp.float32)
    for step in range(1, tp):
        to = (here + step) % tp
        block = lax.dynamic_slice(partial, (0, to * width), (rows, width))
        total = total + rotated(block, "tp", step).astype(jnp.float32)
    return mixed, total.astype(jnp.bfloat16)


def solution(mesh):
    in_specs = (
        P("fsdp", "tp"),
        P(None, "fsdp", "tp"),
        P(None, "tp", None),
        P("tp", None),
        P("fsdp"),
        P("fsdp", "tp"),
    )
    out_specs = (P("fsdp", "tp"), P("fsdp", "tp"))
    return jax.shard_map(shards, mesh=mesh, in_specs=in_specs, out_specs=out_specs, check_vma=False)
```

time: 492 us -> 587 us (1.19)
  matrix products: 84.6 us -> 126 us
  waiting for transfers between devices: 287 us -> 327 us
  other arithmetic: 39.6 us -> 3.12 us
  Pallas kernels: 0 us -> 28.8 us
  local copies, waits for them, and re-layouts: 52.1 us -> 67.5 us
    all_gather x2 -> x6, waiting for transfers between devices: 243 us -> 292 us  [shards(): weights.append(lax.all_gather(part, 'fsdp', axis=1, tiled=True))]
    dot_general x8 -> x20, matrix products: 84.6 us -> 126 us  [the longest x6 51.8 us: shards(): jnp.einsum('jsc,jdc->sd', grad_u, w, preferred_element_type=jnp.float32)]
    reduce_scatter x1 -> x0, waiting for transfers between devices: 37.3 us -> none  [shards(): lax.psum_scatter(partial_value.astype(jnp.bfloat16), 'tp', scatter_dimens...]
    pallas_call x0 -> x6, Pallas kernels: none -> 28.8 us  [convolve(): pl.pallas_call(functools.partial(conv_kernel, rows, taps, short), grid=(w...]
    ppermute x6 -> x7, waiting for transfers between devices: 4.88 us -> 32.8 us  [the longest x2 32.8 us: rotated(): lax.ppermute(value, axis, [(at, (at + steps) % count) for at in range(cou...]
    reshape x1 -> x3, local copies, waits for them, and re-layouts: 0.79 us -> 26.2 us  [the longest x2 25.4 us: toeplitz(): table.astype(long_filter.dtype)]
    while x2 -> x0, local copies, waits for them, and re-layouts: 25.4 us -> none  [blocked_conv(): blocks = lax.map(one_block, (windows, doc_windows, row_docs))]
    add x2 -> x4, other arithmetic: 20.9 us -> 0.16 us  [the longest x1 0.08 us: shards(): sum(((docs[reach + i:reach + i + rows] == doc_ids).astype(jnp.int32) for...]
  transfers between devices with their start and end apart: 9 -> 13, of which waited for: 4 -> 7; matrix products, arithmetic and copies ran while one was open for 13% -> 20% of each run, Pallas kernels for 0% -> 4%
where the time goes in v1:
time: 587 us; the launch traced here: 582 us
  waiting for transfers between devices  327 us (56%)
  matrix products  126 us (21%)
  local copies, waits for them, and re-layouts  67.5 us (11%)
  Pallas kernels  28.8 us (5%)
  between operations  15.1 us (3%)
  starting transfers between devices  14.6 us (2%)
    all_gather x6, waiting for transfers between devices, shards(): weights.append(lax.all_gather(part, 'fsdp', axis=1, tiled=True))  292 us
    dot_general x6, matrix products, shards(): jnp.einsum('jsc,jdc->sd', grad_u, w, preferred_element_type=jnp.float32)  51.8 us
    dot_general x6, matrix products, shards(): jnp.einsum('sd,jdc->jsc', tokens_kv, w[1:], preferred_element_type=jnp.fl...  38.1 us
    ppermute x2, waiting for transfers between devices, rotated(): lax.ppermute(value, axis, [(at, (at + steps) % count) for at in range(cou...  32.8 us
    pallas_call x6, Pallas kernels, convolve(): pl.pallas_call(functools.partial(conv_kernel, rows, taps, short), grid=(w...  28.8 us
    dot_general x6, matrix products, shards(): jnp.dot(tokens_q, w[0], preferred_element_type=jnp.float32)  26.4 us
    reshape x2, local copies, waits for them, and re-layouts, toeplitz(): table.astype(long_filter.dtype)  25.4 us
    unnamed x92, local copies, waits for them, and re-layouts  20.1 us
  transfers between devices with their start and end apart: 13, of which 7 were waited for; matrix products, arithmetic and copies ran while one was open for 20% of the time, Pallas kernels for 4%

profile of v1, /device:TPU:0, one launch (start us, length us, event | category | flops | bytes accessed | tf_op | source)
XLA Modules:
  0.0 581.6 jit_solution(14959810112439717348)
XLA Ops:
  7.2 1.8 fusion.95
  9.1 0.7 all-gather.15.cloned.1.call-update
  9.8 1.8 slice.176
  11.8 3.2 fusion.96
  16.3 2.4 collective-permute-start
  18.7 1.3 collective-permute-start.1
  20.1 5.1 collective-permute-start.4
  25.2 1.3 collective-permute-start.5
  26.5 0.9 slice.147
  27.4 1.3 collective-permute-start.3
  29.1 4.6 convolution_convert_fusion.1
  33.7 0.9 constant_dynamic-update-slice_fusion.2
  34.6 1.1 constant_dynamic-update-slice_fusion.1
  35.7 0.9 constant_dynamic-update-slice_fusion
  36.6 1.5 collective-permute-start.2
  38.1 4.7 convolution_convert_fusion
  42.8 12.9 %copy.12.t_fwd = bf16[128,128,256]{2,1,0:T(8,128)(2,1)} copy(bf16[128,128,256]{0,2,1:T(8,128)(2,1)} %bitcast.116) | data formatting | bytes 16777216 | tf_op jit(solution)/shard_map/reshape | solution.py:45
  55.8 12.5 %copy.13.t_bwd = bf16[128,128,256]{2,1,0:T(8,128)(2,1)} copy(bf16[128,128,256]{0,2,1:T(8,128)(2,1)} %bitcast.117) | data formatting | bytes 16777216 | tf_op jit(solution)/shard_map/reshape | solution.py:45
  68.7 0.8 reshape.51
  70.2 1.1 constant_dynamic-update-slice_fusion.3.grad
  71.4 2.6 broadcast_in_dim.8
  74.0 3.3 constant_dynamic-update-slice_fusion.12
  77.3 8.8 %collective-permute-done.2 = bf16[544,2048]{1,0:T(8,128)(2,1)} collective-permute-done((bf16[544,2048]{1,0:T(8,128)(2,1)}, bf16[544,2048]{1,0:T(8,128)(2,1)}, u32[]{:S(2)}, u32[]{:S(2)}) %collective-permute-start.2) | collective-permute-done | bytes 2228256 | tf_op jit(solution)/shard_map/ppermute | solution.py:22
  86.1 3.3 constant_dynamic-update-slice_fusion.11
  89.5 3.4 fusion.87.u_q
  92.9 3.2 fusion.78.u_kv
  96.5 3.4 copy-done.3
  99.9 1.6 shard_map.82
  102.2 6.8 %all-gather.15.cloned.1.call-done = bf16[3,4096,128]{2,1,0:T(8,128)(2,1)} async-done(((bf16[3,256,128]{2,1,0:T(8,128)(2,1)}), bf16[3,4096,128]{2,1,0:T(8,128)(2,1)}) %all-gather.15.cloned.1.call-update) | async-done | bytes 3145744 | tf_op jit(solution)/shard_map/all_gather | solution.py:180
  109.0 3.4 fusion.84.u_q
  112.4 3.2 fusion.81.u_kv
  115.9 3.8 copy-done.4
  119.7 1.7 shard_map.81
  121.6 3.2 convolution_bitcast_fusion.3
  124.8 3.2 convolution_bitcast_fusion.4
  128.0 43.9 %all-gather.13.cloned.1.call-done = bf16[3,4096,256]{2,1,0:T(8,128)(2,1)} async-done(((bf16[3,256,256]{2,1,0:T(8,128)(2,1)}), bf16[3,4096,256]{2,1,0:T(8,128)(2,1)}) %all-gather.13.cloned.1.call-update) | async-done | bytes 6291472 | tf_op jit(solution)/shard_map/all_gather | solution.py:180
  171.9 3.8 fusion.69.u_q
  175.8 5.8 %fusion.66.u_kv = bf16[2,416,256]{2,1,0:T(8,128)(2,1)S(1)} fusion(bf16[3,4096,256]{2,1,0:T(8,128)(2,1)} %all-gather.13.cloned.1.call-done, bf16[544,4096]{1,0:T(8,128)(2,1)} %constant_dynamic-update-slice_fusion.11), kind=kOutput, calls=%fused_computation.60 | convolution fusion | flops 1745043456 | bytes 8028160 | tf_op jit(solution)/shard_map/sd,jdc->jsc/dot_general | solution.py:225
  181.7 0.7 slice-done.11
  182.3 3.6 shard_map.80
  186.0 3.9 convolution_bitcast_fusion.5
  189.9 84.1 %all-gather.11.cloned.1.call-done = bf16[3,4096,512]{2,1,0:T(8,128)(2,1)} async-done(((bf16[3,256,512]{2,1,0:T(8,128)(2,1)}), bf16[3,4096,512]{2,1,0:T(8,128)(2,1)}) %all-gather.11.cloned.1.call-update) | async-done | bytes 12582928 | tf_op jit(solution)/shard_map/all_gather | solution.py:180
  274.0 5.3 fusion.60.u_q
  279.3 8.8 %fusion.45.u_kv = bf16[2,416,512]{2,1,0:T(8,128)(2,1)S(1)} fusion(bf16[3,4096,512]{2,1,0:T(8,128)(2,1)} %all-gather.11.cloned.1.call-done, bf16[544,4096]{1,0:T(8,128)(2,1)} %constant_dynamic-update-slice_fusion.11), kind=kOutput, calls=%fused_computation.53 | convolution fusion | flops 3490086912 | bytes 12648448 | tf_op jit(solution)/shard_map/sd,jdc->jsc/dot_general | solution.py:225
  288.1 7.3 %shard_map.79 = (bf16[256,512]{1,0:T(8,128)(2,1)S(1)}, bf16[3,256,512]{2,1,0:T(8,128)(2,1)S(1)}) custom-call(bf16[416,512]{1,0:T(8,128)(2,1)S(1)} %fusion.60.u_q, bf16[2,416,512]{2,1,0:T(8,128)(2,1)S(1)} %fusion.45.u_kv, bf16[400,2048]{1,0:T(8,128)(2,1)S(1)} %constant_dynamic-update-slice_fusion.3.grad, f32[3,8,2048]{2,1,0:T(8,128)S(1)} %pad.5.filters, ...), custom_call_target="tpu_custom_call" | custom-call | flops 1073741824 | bytes 5242880 | tf_op jit(solution)/shard_map/pallas_call | solution.py:119
  295.4 0.9 copy-done.10
  296.3 79.3 %all-gather.9.cloned.1.call-done = bf16[3,4096,512]{2,1,0:T(8,128)(2,1)} async-done(((bf16[3,256,512]{2,1,0:T(8,128)(2,1)}), bf16[3,4096,512]{2,1,0:T(8,128)(2,1)}) %all-gather.9.cloned.1.call-update) | async-done | bytes 12582928 | tf_op jit(solution)/shard_map/all_gather | solution.py:180
  375.6 5.3 fusion.57.u_q
  380.9 9.0 %fusion.48.u_kv = bf16[2,416,512]{2,1,0:T(8,128)(2,1)S(1)} fusion(bf16[3,4096,512]{2,1,0:T(8,128)(2,1)} %all-gather.9.cloned.1.call-done, bf16[544,4096]{1,0:T(8,128)(2,1)} %constant_dynamic-update-slice_fusion.11), kind=kOutput, calls=%fused_computation.54 | convolution fusion | flops 3490086912 | bytes 12648448 | tf_op jit(solution)/shard_map/sd,jdc->jsc/dot_general | solution.py:225
  390.0 7.5 %shard_map.78 = (bf16[256,512]{1,0:T(8,128)(2,1)S(1)}, bf16[3,256,512]{2,1,0:T(8,128)(2,1)S(1)}) custom-call(bf16[416,512]{1,0:T(8,128)(2,1)S(1)} %fusion.57.u_q, bf16[2,416,512]{2,1,0:T(8,128)(2,1)S(1)} %fusion.48.u_kv, bf16[400,2048]{1,0:T(8,128)(2,1)S(1)} %constant_dynamic-update-slice_fusion.3.grad, f32[3,8,2048]{2,1,0:T(8,128)S(1)} %pad.5.filters, ...), custom_call_target="tpu_custom_call" | custom-call | flops 1073741824 | bytes 5242880 | tf_op jit(solution)/shard_map/pallas_call | solution.py:119
  397.4 0.9 copy-done.12
  398.3 78.3 %all-gather.7.cloned.1.call-done = bf16[3,4096,512]{2,1,0:T(8,128)(2,1)} async-done(((bf16[3,256,512]{2,1,0:T(8,128)(2,1)}), bf16[3,4096,512]{2,1,0:T(8,128)(2,1)}) %all-gather.7.cloned.1.call-update) | async-done | bytes 12582928 | tf_op jit(solution)/shard_map/all_gather | solution.py:180
  476.6 8.1 %fusion.51.u_kv = bf16[2,416,512]{2,1,0:T(8,128)(2,1)S(1)} fusion(bf16[3,4096,512]{2,1,0:T(8,128)(2,1)} %all-gather.7.cloned.1.call-done, bf16[544,4096]{1,0:T(8,128)(2,1)} %constant_dynamic-update-slice_fusion.11), kind=kOutput, calls=%fused_computation.55 | convolution fusion | flops 3490086912 | bytes 12648448 | tf_op jit(solution)/shard_map/sd,jdc->jsc/dot_general | solution.py:225
  484.7 5.1 fusion.54.u_q
  489.9 3.4 copy-done.2
  493.2 3.4 copy-done.5
  496.6 7.2 %shard_map.77 = (bf16[256,512]{1,0:T(8,128)(2,1)S(1)}, bf16[3,256,512]{2,1,0:T(8,128)(2,1)S(1)}) custom-call(bf16[416,512]{1,0:T(8,128)(2,1)S(1)} %fusion.54.u_q, bf16[2,416,512]{2,1,0:T(8,128)(2,1)S(1)} %fusion.51.u_kv, bf16[400,2048]{1,0:T(8,128)(2,1)S(1)} %constant_dynamic-update-slice_fusion.3.grad, f32[3,8,2048]{2,1,0:T(8,128)S(1)} %pad.5.filters, ...), custom_call_target="tpu_custom_call" | custom-call | flops 1073741824 | bytes 5242880 | tf_op jit(solution)/shard_map/pallas_call | solution.py:119
  503.9 14.4 %convolution_bitcast_fusion = f32[256,4096]{1,0:T(8,128)} fusion(bf16[3,256,512]{2,1,0:T(8,128)(2,1)S(1)} %copy-done.11, bf16[3,4096,512]{2,1,0:T(8,128)(2,1)} %all-gather.11.cloned.1.call-done), kind=kOutput, calls=%fused_computation.14 | convolution fusion | flops 3221225472 | bytes 17563648 | tf_op jit(solution)/shard_map/jsc,jdc->sd/dot_general | solution.py:232
  518.2 14.3 %convolution_bitcast_fusion.1 = f32[256,4096]{1,0:T(8,128)} fusion(bf16[3,256,512]{2,1,0:T(8,128)(2,1)S(1)} %copy-done.13, bf16[3,4096,512]{2,1,0:T(8,128)(2,1)} %all-gather.9.cloned.1.call-done), kind=kOutput, calls=%fused_computation.15 | convolution fusion | flops 3221225472 | bytes 17563648 | tf_op jit(solution)/shard_map/jsc,jdc->sd/dot_general | solution.py:232
  532.5 12.8 %fusion.17 = bf16[256,4096]{1,0:T(8,128)(2,1)S(1)} fusion(f32[256,4096]{1,0:T(8,128)} %convolution_bitcast_fusion.3, f32[256,4096]{1,0:T(8,128)} %convolution_bitcast_fusion.4, f32[256,4096]{1,0:T(8,128)} %convolution_bitcast_fusion.5, f32[256,4096]{1,0:T(8,128)} %convolution_bitcast_fusion, f32[256,4096]{1,0:T(8,128)} %convolution_bitcast_fusion.1, ...), kind=kOutput, calls=%fused_computation.25 | convolution fusion | flops 3227516928 | bytes 36438016 | tf_op jit(solution)/shard_map/jsc,jdc->sd/dot_general | solution.py:232
  545.3 1.0 constant_dynamic-slice_fusion
  546.3 1.5 collective-permute-start.6
  548.0 24.0 %collective-permute-done.6 = bf16[256,2048]{1,0:T(8,128)(2,1)} collective-permute-done((bf16[256,2048]{1,0:T(8,128)(2,1)}, bf16[256,2048]{1,0:T(8,128)(2,1)}, u32[]{:S(2)}, u32[]{:S(2)}) %collective-permute-start.6) | collective-permute-done | bytes 1048608 | tf_op jit(solution)/shard_map/ppermute | solution.py:22
  572.0 2.6 add_convert_fusion
  (128 shorter events, 4.8 us)
Async XLA Ops:
  7.2 21.9 %copy-start = (bf16[128,128]{1,0:T(8,128)(2,1)S(1)}, bf16[128,128]{1,0:T(8,128)(2,1)}, u32[]{:S(2)}) copy-start(bf16[128,128]{1,0:T(8,128)(2,1)} %param.9) | copy-start | bytes 98308
  7.2 82.3 %all-gather.17.cloned.1.call-start = ((), (), s32[]{:S(2)}) async-start(), calls=%async_computation.5 | async-start | bytes 3342336 | tf_op jit(solution)/shard_map/all_gather | solution.py:180
  9.0 99.9 %all-gather.15.cloned.1.call-start = ((), (), s32[]{:S(2)}) async-start(), calls=%async_computation.4 | async-start | bytes 3342336 | tf_op jit(solution)/shard_map/all_gather | solution.py:180
  9.1 7.0 %copy-start.14 = (bf16[256,2048]{1,0:T(8,128)(2,1)S(1)}, bf16[256,2048]{1,0:T(8,128)(2,1)}, u32[]{:S(2)}) copy-start(bf16[256,2048]{1,0:T(8,128)(2,1)} %param.6) | copy-start | bytes 3145732
  9.8 162.1 %all-gather.13.cloned.1.call-start = ((), (), s32[]{:S(2)}) async-start(), calls=%async_computation.3 | async-start | bytes 6684672 | tf_op jit(solution)/shard_map/all_gather | solution.py:180
  11.7 8.3 %copy-start.21 = (s32[256]{0:T(256)S(1)}, s32[256]{0:T(256)}, u32[]{:S(2)}) copy-start(s32[256]{0:T(256)} %param.10) | copy-start | bytes 3076
  11.7 14.8 %copy-start.18 = (bf16[256,2048]{1,0:T(8,128)(2,1)S(1)}, bf16[256,2048]{1,0:T(8,128)(2,1)}, u32[]{:S(2)}) copy-start(bf16[256,2048]{1,0:T(8,128)(2,1)} %param.11) | copy-start | bytes 3145732
  11.7 262.2 %all-gather.11.cloned.1.call-start = ((), (), s32[]{:S(2)}) async-start(), calls=%async_computation.2 | async-start | bytes 13369344 | tf_op jit(solution)/shard_map/all_gather | solution.py:180
  15.0 360.6 %all-gather.9.cloned.1.call-start = ((), (), s32[]{:S(2)}) async-start(), calls=%async_computation.1 | async-start | bytes 13369344 | tf_op jit(solution)/shard_map/all_gather | solution.py:180
  15.6 461.0 %all-gather.7.cloned.1.call-start = ((), (), s32[]{:S(2)}) async-start(), calls=%async_computation | async-start | bytes 13369344 | tf_op jit(solution)/shard_map/all_gather | solution.py:180
  16.3 17.5 %collective-permute-start = (bf16[144,2048]{1,0:T(8,128)(2,1)S(1)}, bf16[144,2048]{1,0:T(8,128)(2,1)S(1)}, u32[]{:S(2)}, u32[]{:S(2)}) collective-permute-start(bf16[144,2048]{1,0:T(8,128)(2,1)S(1)} %get-tuple-element.32), channel_id=1, source_target_pairs={{0,2},{2,4},{4,6},{6,8},{8,10},{10,12},{12,14},{14,16},{16,18},{18... | collective-permute-start | bytes 1769480 | tf_op jit(solution)/shard_map/ppermute | solution.py:17
  18.7 17.1 %collective-permute-start.1 = (bf16[144,2048]{1,0:T(8,128)(2,1)S(1)}, bf16[144,2048]{1,0:T(8,128)(2,1)S(1)}, u32[]{:S(2)}, u32[]{:S(2)}) collective-permute-start(bf16[144,2048]{1,0:T(8,128)(2,1)S(1)} %get-tuple-element.31), channel_id=1, source_target_pairs={{2,0},{4,2},{6,4},{8,6},{10,8},{12,10},{14,12},{16,14},{18,16},{20... | collective-permute-start | bytes 1769480 | tf_op jit(solution)/shard_map/ppermute | solution.py:17
  20.1 49.5 %collective-permute-start.4 = (s32[144]{0:T(256)S(1)}, s32[144]{0:T(256)S(1)}, u32[]{:S(2)}, u32[]{:S(2)}) collective-permute-start(s32[144]{0:T(256)S(1)} %get-tuple-element.44), channel_id=1, source_target_pairs={{0,2},{2,4},{4,6},{6,8},{8,10},{10,12},{12,14},{14,16},{16,18},{18... | collective-permute-start | bytes 1736 | tf_op jit(solution)/shard_map/ppermute | solution.py:17
  25.2 44.4 %collective-permute-start.5 = (s32[144]{0:T(256)S(1)}, s32[144]{0:T(256)S(1)}, u32[]{:S(2)}, u32[]{:S(2)}) collective-permute-start(s32[144]{0:T(256)S(1)} %get-tuple-element.45), channel_id=1, source_target_pairs={{2,0},{4,2},{6,4},{8,6},{10,8},{12,10},{14,12},{16,14},{18,16},{20... | collective-permute-start | bytes 1736 | tf_op jit(solution)/shard_map/ppermute | solution.py:17
  27.4 42.9 %collective-permute-start.3 = (bf16[144,2048]{1,0:T(8,128)(2,1)}, bf16[144,2048]{1,0:T(8,128)(2,1)}, u32[]{:S(2)}, u32[]{:S(2)}) collective-permute-start(bf16[144,2048]{1,0:T(8,128)(2,1)} %slice.147), channel_id=1, source_target_pairs={{2,0},{4,2},{6,4},{8,6},{10,8},{12,10},{14,12},{16,14},{18,16},{20... | collective-permute-start | bytes 1769480 | tf_op jit(solution)/shard_map/ppermute | solution.py:17
  36.6 49.5 %collective-permute-start.2 = (bf16[544,2048]{1,0:T(8,128)(2,1)}, bf16[544,2048]{1,0:T(8,128)(2,1)}, u32[]{:S(2)}, u32[]{:S(2)}) collective-permute-start(bf16[544,2048]{1,0:T(8,128)(2,1)} %constant_dynamic-update-slice_fusion), channel_id=1, source_target_pairs={{0,1},{1,0},{2,3},{3,2},{4,5},{5,4},{6,7},{7,6},{8,9},{9,8},{10,11... | collective-permute-start | bytes 6684680 | tf_op jit(solution)/shard_map/ppermute | solution.py:22
  55.8 12.5 %copy-start.20 = (f32[3,128,7]{1,2,0:T(8,128)S(1)}, f32[3,128,7]{1,2,0:T(8,128)}, u32[]{:S(2)}) copy-start(f32[3,128,7]{1,2,0:T(8,128)} %param.8) | copy-start | bytes 32260
  89.5 3.5 copy-start.15
  89.5 6.9 %slice-start = ((s8[8388608]{0:T(1024)(128)(4,1)}), s8[4194304]{0:T(1024)(128)(4,1)S(1)}, s32[]{:S(2)}) async-start(s8[8388608]{0:T(1024)(128)(4,1)} %bitcast.100), calls=%async_computation.6 | async-start | bytes 8388608
  92.9 3.6 slice-start.1
  96.5 3.4 copy-start.3
  101.6 0.6 copy-start.6
  109.0 3.5 copy-start.17
  109.0 6.7 %slice-start.2 = ((s8[8388608]{0:T(1024)(128)(4,1)}), s8[4194304]{0:T(1024)(128)(4,1)S(1)}, s32[]{:S(2)}) async-start(s8[8388608]{0:T(1024)(128)(4,1)} %bitcast.102), calls=%async_computation.8 | async-start | bytes 8388608
  112.4 3.5 slice-start.3
  115.9 3.8 copy-start.4
  119.7 1.9 copy-start.16
  121.4 3.5 copy-start.8
  171.9 9.7 %slice-start.4 = ((s8[8388608]{0:T(1024)(128)(4,1)}), s8[4194304]{0:T(1024)(128)(4,1)S(1)}, s32[]{:S(2)}) async-start(s8[8388608]{0:T(1024)(128)(4,1)} %bitcast.104), calls=%async_computation.10 | async-start | bytes 8388608
  171.9 9.7 %slice-start.10 = ((s8[8388608]{0:T(1024)(128)(4,1)}), s8[4194304]{0:T(1024)(128)(4,1)S(1)}, s32[]{:S(2)}) async-start(s8[8388608]{0:T(1024)(128)(4,1)} %bitcast.110), calls=%async_computation.16 | async-start | bytes 8388608
  175.8 5.9 %slice-start.5 = ((s8[8388608]{0:T(1024)(128)(4,1)}), s8[4194304]{0:T(1024)(128)(4,1)S(1)}, s32[]{:S(2)}) async-start(s8[8388608]{0:T(1024)(128)(4,1)} %bitcast.104), calls=%async_computation.11 | async-start | bytes 8388608
  175.8 6.6 %slice-start.11 = ((s8[8388608]{0:T(1024)(128)(4,1)}), s8[4194304]{0:T(1024)(128)(4,1)S(1)}, s32[]{:S(2)}) async-start(s8[8388608]{0:T(1024)(128)(4,1)} %bitcast.110), calls=%async_computation.17 | async-start | bytes 8388608
  175.8 10.2 %slice-start.16 = ((s8[6291456]{0:T(1024)(128)(4,1)}), s8[4194304]{0:T(1024)(128)(4,1)S(1)}, s32[]{:S(2)}) async-start(s8[6291456]{0:T(1024)(128)(4,1)} %bitcast.118), calls=%async_computation.22 | async-start | bytes 8388608
  182.3 3.6 slice-start.17
  274.0 14.1 %slice-start.6 = ((s8[8388608]{0:T(1024)(128)(4,1)}), s8[4194304]{0:T(1024)(128)(4,1)S(1)}, s32[]{:S(2)}) async-start(s8[8388608]{0:T(1024)(128)(4,1)} %bitcast.106), calls=%async_computation.12 | async-start | bytes 8388608
  274.0 14.1 %slice-start.12 = ((s8[8388608]{0:T(1024)(128)(4,1)}), s8[4194304]{0:T(1024)(128)(4,1)S(1)}, s32[]{:S(2)}) async-start(s8[8388608]{0:T(1024)(128)(4,1)} %bitcast.112), calls=%async_computation.18 | async-start | bytes 8388608
  279.2 8.9 %slice-start.7 = ((s8[8388608]{0:T(1024)(128)(4,1)}), s8[4194304]{0:T(1024)(128)(4,1)S(1)}, s32[]{:S(2)}) async-start(s8[8388608]{0:T(1024)(128)(4,1)} %bitcast.106), calls=%async_computation.13 | async-start | bytes 8388608
  279.3 8.9 %slice-start.13 = ((s8[8388608]{0:T(1024)(128)(4,1)}), s8[4194304]{0:T(1024)(128)(4,1)S(1)}, s32[]{:S(2)}) async-start(s8[8388608]{0:T(1024)(128)(4,1)} %bitcast.112), calls=%async_computation.19 | async-start | bytes 8388608
  295.4 0.9 copy-start.10
  375.6 14.4 %slice-start.8 = ((s8[8388608]{0:T(1024)(128)(4,1)}), s8[4194304]{0:T(1024)(128)(4,1)S(1)}, s32[]{:S(2)}) async-start(s8[8388608]{0:T(1024)(128)(4,1)} %bitcast.108), calls=%async_computation.14 | async-start | bytes 8388608
  375.6 14.4 %slice-start.14 = ((s8[8388608]{0:T(1024)(128)(4,1)}), s8[4194304]{0:T(1024)(128)(4,1)S(1)}, s32[]{:S(2)}) async-start(s8[8388608]{0:T(1024)(128)(4,1)} %bitcast.114), calls=%async_computation.20 | async-start | bytes 8388608
  380.9 9.1 %slice-start.9 = ((s8[8388608]{0:T(1024)(128)(4,1)}), s8[4194304]{0:T(1024)(128)(4,1)S(1)}, s32[]{:S(2)}) async-start(s8[8388608]{0:T(1024)(128)(4,1)} %bitcast.108), calls=%async_computation.15 | async-start | bytes 8388608
  380.9 9.1 %slice-start.15 = ((s8[8388608]{0:T(1024)(128)(4,1)}), s8[4194304]{0:T(1024)(128)(4,1)S(1)}, s32[]{:S(2)}) async-start(s8[8388608]{0:T(1024)(128)(4,1)} %bitcast.114), calls=%async_computation.21 | async-start | bytes 8388608
  397.4 0.9 copy-start.12
  489.8 3.4 copy-start.2
  493.2 3.4 copy-start.5
  496.6 7.2 %copy-start.11 = (bf16[3,256,512]{2,1,0:T(8,128)(2,1)S(1)}, bf16[3,256,512]{2,1,0:T(8,128)(2,1)}, u32[]{:S(2)}) copy-start(bf16[3,256,512]{2,1,0:T(8,128)(2,1)} %copy-done.10) | copy-start | bytes 2359300
  503.8 14.4 %copy-start.13 = (bf16[3,256,512]{2,1,0:T(8,128)(2,1)S(1)}, bf16[3,256,512]{2,1,0:T(8,128)(2,1)}, u32[]{:S(2)}) copy-start(bf16[3,256,512]{2,1,0:T(8,128)(2,1)} %copy-done.12) | copy-start | bytes 2359300
  532.5 15.4 %copy-start.9 = (bf16[256,128]{1,0:T(8,128)(2,1)S(1)}, bf16[256,128]{1,0:T(8,128)(2,1)}, u32[]{:S(2)}) copy-start(bf16[256,128]{1,0:T(8,128)(2,1)} %copy-done.8) | copy-start | bytes 196612
  532.5 15.4 %copy-start.7 = (bf16[256,128]{1,0:T(8,128)(2,1)S(1)}, bf16[256,128]{1,0:T(8,128)(2,1)}, u32[]{:S(2)}) copy-start(bf16[256,128]{1,0:T(8,128)(2,1)} %copy-done.6) | copy-start | bytes 196612
  532.5 42.0 %copy-start.1 = (bf16[128,128]{1,0:T(8,128)(2,1)S(1)}, bf16[128,128]{1,0:T(8,128)(2,1)}, u32[]{:S(2)}) copy-start(bf16[128,128]{1,0:T(8,128)(2,1)} %param.9) | copy-start | bytes 98308
  546.3 25.6 %collective-permute-start.6 = (bf16[256,2048]{1,0:T(8,128)(2,1)}, bf16[256,2048]{1,0:T(8,128)(2,1)}, u32[]{:S(2)}, u32[]{:S(2)}) collective-permute-start(bf16[256,2048]{1,0:T(8,128)(2,1)} %constant_dynamic-slice_fusion), channel_id=1, source_target_pairs={{0,1},{1,0},{2,3},{3,2},{4,5},{5,4},{6,7},{7,6},{8,9},{9,8},{10,11... | collective-permute-start | bytes 3145736 | tf_op jit(solution)/shard_map/ppermute | solution.py:22
  548.0 26.6 %copy-start.19 = (bf16[256,2048]{1,0:T(8,128)(2,1)}, bf16[256,2048]{1,0:T(8,128)(2,1)S(1)}, u32[]{:S(2)}) copy-start(bf16[256,2048]{1,0:T(8,128)(2,1)S(1)} %constant_dynamic-update-slice_fusion.5) | copy-start | bytes 3145732
Sparse Core Ops, SparseCore 0:
  10.2 51.8 all-gather.16
  64.3 44.5 all-gather.14
  111.1 60.7 all-gather.12
  174.5 99.3 all-gather.10
  276.6 98.9 all-gather.8
  377.6 98.9 all-gather.6

commit v2 on v1

--- a/solution.py
+++ b/solution.py
@@ -154,14 +154,8 @@
 
 
 def chunk_sizes(width):
-    units = width // LANES
-    sizes = []
-    left = units
-    while left > 0:
-        size = max(1, min(units // 4, (left + 1) // 2))
-        sizes.append(size * LANES)
-        left -= size
-    return sizes
+    last = max(1, width // LANES // 4) * LANES
+    return [size for size in (width - last, last) if size > 0]
 
 
 def shards(tokens, w_feat, short_filter, long_filter, doc_ids, grad_out):
@@ -221,6 +215,8 @@
     tokens_q = tokens_ext[taps:]
     mixed, partial, start = [], None, 0
     for size, w in zip(sizes, weights):
+        if partial is not None:
+            w, partial = lax.optimization_barrier((w, partial))
         u_q = jnp.dot(tokens_q, w[0], preferred_element_type=jnp.float32).astype(jnp.bfloat16)
         u_kv = jnp.einsum(
             "sd,jdc->jsc", tokens_kv, w[1:], preferred_element_type=jnp.float32

time: 587 us -> 401 us (0.68)
  waiting for transfers between devices: 327 us -> 191 us
  matrix products: 126 us -> 81.2 us
    all_gather x6 -> x2, waiting for transfers between devices: 292 us -> 167 us  [shards(): weights.append(lax.all_gather(part, 'fsdp', axis=1, tiled=True))]
    dot_general x6 -> x2, matrix products: 51.8 us -> 32.5 us  [shards(): jnp.einsum('jsc,jdc->sd', grad_u, w, preferred_element_type=jnp.float32)]
    dot_general x6 -> x2, matrix products: 38.1 us -> 24.8 us  [shards(): jnp.einsum('sd,jdc->jsc', tokens_kv, w[1:], preferred_element_type=jnp.fl...]
    dot_general x6 -> x2, matrix products: 26.4 us -> 14.6 us  [shards(): jnp.dot(tokens_q, w[0], preferred_element_type=jnp.float32)]
    ppermute x2, waiting for transfers between devices: 32.8 us -> 24.4 us  [rotated(): lax.ppermute(value, axis, [(at, (at + steps) % count) for at in range(cou...]
    unnamed x92 -> x45, local copies, waits for them, and re-layouts: 20.1 us -> 18.7 us
    pallas_call x6 -> x2, Pallas kernels: 28.8 us -> 28.5 us  [convolve(): pl.pallas_call(functools.partial(conv_kernel, rows, taps, short), grid=(w...]
  transfers between devices with their start and end apart: 13 -> 9, of which waited for: 7 -> 4; matrix products, arithmetic and copies ran while one was open for 20% -> 25% of each run, Pallas kernels for 4% -> 5%
where the time goes in v2:
time: 401 us; the launch traced here: 400 us
  waiting for transfers between devices  191 us (48%)
  matrix products  81.2 us (20%)
  local copies, waits for them, and re-layouts  65.1 us (16%)
  Pallas kernels  28.5 us (7%)
  starting transfers between devices  14.4 us (4%)
  between operations  14.4 us (4%)
  other arithmetic  4.88 us (1%)
    all_gather x2, waiting for transfers between devices, shards(): weights.append(lax.all_gather(part, 'fsdp', axis=1, tiled=True))  167 us
    dot_general x2, matrix products, shards(): jnp.einsum('jsc,jdc->sd', grad_u, w, preferred_element_type=jnp.float32)  32.5 us
    pallas_call x2, Pallas kernels, convolve(): pl.pallas_call(functools.partial(conv_kernel, rows, taps, short), grid=(w...  28.5 us
    reshape x2, local copies, waits for them, and re-layouts, toeplitz(): table.astype(long_filter.dtype)  25.9 us
    dot_general x2, matrix products, shards(): jnp.einsum('sd,jdc->jsc', tokens_kv, w[1:], preferred_element_type=jnp.fl...  24.8 us
    ppermute x2, waiting for transfers between devices, rotated(): lax.ppermute(value, axis, [(at, (at + steps) % count) for at in range(cou...  24.4 us
    unnamed x45, local copies, waits for them, and re-layouts  18.7 us
    dot_general x2, matrix products, shards(): jnp.dot(tokens_q, w[0], preferred_element_type=jnp.float32)  14.6 us
  transfers between devices with their start and end apart: 9, of which 4 were waited for; matrix products, arithmetic and copies ran while one was open for 25% of the time, Pallas kernels for 5%

profile of v2, /device:TPU:0, one launch (start us, length us, event | category | flops | bytes accessed | tf_op | source)
XLA Modules:
  0.0 400.0 jit_solution(2536970921891128514)
XLA Ops:
  7.2 0.0 all-gather.3.cloned.1.call-start
  7.2 3.3 slice.107
  10.5 0.0 all-gather.3.cloned.1.call-update
  10.5 0.0 all-gather.5.cloned.1.call-start
  10.6 2.1 slice.134
  12.8 0.1 fusion.43
  12.9 2.4 collective-permute-start
  15.3 1.3 collective-permute-start.1
  16.6 0.1 fusion.46
  16.7 5.1 %collective-permute-start.4 = (s32[144]{0:T(256)S(1)}, s32[144]{0:T(256)S(1)}, u32[]{:S(2)}, u32[]{:S(2)}) collective-permute-start(s32[144]{0:T(256)S(1)} %get-tuple-element.27), channel_id=1, source_target_pairs={{0,2},{2,4},{4,6},{6,8},{8,10},{10,12},{12,14},{14,16},{16,18},{18... | collective-permute-start | bytes 1736 | tf_op jit(solution)/shard_map/ppermute | solution.py:17
  21.8 1.3 collective-permute-start.5
  23.1 0.9 slice.111
  24.0 1.3 collective-permute-start.3
  25.3 0.1 copy.14
  25.4 0.1 copy.15
  25.5 0.2 iota.51
  25.7 4.6 %convolution_convert_fusion.1 = bf16[32768,128]{1,0:T(8,128)(2,1)} fusion(bf16[128,128]{1,0:T(8,128)(2,1)S(1)} %copy-done, s32[32768]{0:T(1024)S(1)} %get-tuple-element.17), kind=kOutput, calls=%fused_computation.1 | convolution fusion | flops 1086324736 | bytes 8552448 | tf_op jit(solution)/shard_map/dot_general | solution.py:44
  30.3 0.9 constant_dynamic-update-slice_fusion.2
  31.2 1.1 constant_dynamic-update-slice_fusion.1
  32.3 0.9 constant_dynamic-update-slice_fusion
  33.1 1.5 collective-permute-start.2
  34.6 4.6 %convolution_convert_fusion = bf16[32768,128]{1,0:T(8,128)(2,1)} fusion(bf16[128,128]{1,0:T(8,128)(2,1)S(1)} %copy-done, s32[32768]{0:T(1024)S(1)} %get-tuple-element.16), kind=kOutput, calls=%fused_computation | convolution fusion | flops 1086324736 | bytes 8552448 | tf_op jit(solution)/shard_map/dot_general | solution.py:44
  39.2 12.9 %copy.12.t_fwd = bf16[128,128,256]{2,1,0:T(8,128)(2,1)} copy(bf16[128,128,256]{0,2,1:T(8,128)(2,1)} %bitcast.52) | data formatting | bytes 16777216 | tf_op jit(solution)/shard_map/reshape | solution.py:45
  52.1 0.1 constant_dynamic-update-slice_fusion.4
  52.2 13.0 %copy.13.t_bwd = bf16[128,128,256]{2,1,0:T(8,128)(2,1)} copy(bf16[128,128,256]{0,2,1:T(8,128)(2,1)} %bitcast.53) | data formatting | bytes 16777216 | tf_op jit(solution)/shard_map/reshape | solution.py:45
  65.2 0.4 broadcast_in_dim.9
  65.6 0.8 reshape.51
  66.5 0.1 add_add_fusion
  66.5 0.1 slice.118
  66.6 0.1 fusion.42
  66.7 0.1 broadcast_compare_fusion.4
  66.8 0.1 fusion.45
  66.9 0.1 broadcast_compare_fusion.1
  67.0 0.7 add_convert_fusion.1
  67.7 0.1 convert_add_fusion
  67.8 1.1 constant_dynamic-update-slice_fusion.3.grad
  68.9 2.6 broadcast_in_dim.8
  71.5 3.2 constant_dynamic-update-slice_fusion.6
  74.8 1.3 collective-permute-done.2
  76.1 3.3 constant_dynamic-update-slice_fusion.5
  79.4 134.9 %all-gather.3.cloned.1.call-done = bf16[3,4096,1536]{2,1,0:T(8,128)(2,1)} async-done(((bf16[3,256,1536]{2,1,0:T(8,128)(2,1)}), bf16[3,4096,1536]{2,1,0:T(8,128)(2,1)}) %all-gather.3.cloned.1.call-update) | async-done | bytes 37748752 | tf_op jit(solution)/shard_map/all_gather | solution.py:174
  214.4 9.4 %fusion.24.u_q = bf16[416,1536]{1,0:T(8,128)(2,1)S(1)} fusion(bf16[3,4096,1536]{2,1,0:T(8,128)(2,1)} %all-gather.3.cloned.1.call-done, bf16[544,4096]{1,0:T(8,128)(2,1)} %constant_dynamic-update-slice_fusion.5), kind=kOutput, calls=%fused_computation.26 | convolution fusion | flops 5235130368 | bytes 17268736 | tf_op jit(solution)/shard_map/dot_general | solution.py:220
  223.8 16.8 %fusion.19.u_kv = bf16[2,416,1536]{2,1,0:T(8,128)(2,1)S(1)} fusion(bf16[3,4096,1536]{2,1,0:T(8,128)(2,1)} %all-gather.3.cloned.1.call-done, bf16[544,4096]{1,0:T(8,128)(2,1)} %constant_dynamic-update-slice_fusion.5), kind=kOutput, calls=%fused_computation.23 | convolution fusion | flops 10470260736 | bytes 31129600 | tf_op jit(solution)/shard_map/sd,jdc->jsc/dot_general | solution.py:221
  240.6 0.1 broadcast_in_dim.11.ahead
  240.7 0.1 broadcast_in_dim.10.back
  240.8 3.4 copy-done.2
  244.2 3.4 copy-done.4
  247.6 21.4 %shard_map.77 = (bf16[256,1536]{1,0:T(8,128)(2,1)S(1)}, bf16[3,256,1536]{2,1,0:T(8,128)(2,1)S(1)}) custom-call(bf16[416,1536]{1,0:T(8,128)(2,1)S(1)} %fusion.24.u_q, bf16[2,416,1536]{2,1,0:T(8,128)(2,1)S(1)} %fusion.19.u_kv, bf16[400,2048]{1,0:T(8,128)(2,1)S(1)} %constant_dynamic-update-slice_fusion.3.grad, f32[3,8,2048]{2,1,0:T(8,128)S(1)} %pad.5.filters, ...), custom_call_target="tpu_custom_call" | custom-call | flops 3221225472 | bytes 15728640 | tf_op jit(solution)/shard_map/pallas_call | solution.py:119
  269.1 0.9 copy-done.10
  269.9 1.4 copy-done.14
  271.3 18.9 %convolution_bitcast_fusion.1 = f32[256,4096]{1,0:T(8,128)} fusion(bf16[3,256,1536]{2,1,0:T(8,128)(2,1)} %copy-done.14, bf16[3,4096,1536]{2,1,0:T(8,128)(2,1)} %all-gather.3.cloned.1.call-done), kind=kOutput, calls=%fused_computation.15 | convolution fusion | flops 9663676416 | bytes 44302336 | tf_op jit(solution)/shard_map/jsc,jdc->sd/dot_general | solution.py:228
  290.2 32.1 %all-gather.5.cloned.1.call-done = bf16[3,4096,512]{2,1,0:T(8,128)(2,1)} async-done(((bf16[3,256,512]{2,1,0:T(8,128)(2,1)}), bf16[3,4096,512]{2,1,0:T(8,128)(2,1)}) %all-gather.5.cloned.1.call-update) | async-done | bytes 12582928 | tf_op jit(solution)/shard_map/all_gather | solution.py:174
  322.3 8.1 %fusion.30.u_kv = bf16[2,416,512]{2,1,0:T(8,128)(2,1)S(1)} fusion(bf16[3,4096,512]{2,1,0:T(8,128)(2,1)} %all-gather.5.cloned.1.call-done, bf16[544,4096]{1,0:T(8,128)(2,1)} %constant_dynamic-update-slice_fusion.5), kind=kOutput, calls=%fused_computation.29 | convolution fusion | flops 3490086912 | bytes 12648448 | tf_op jit(solution)/shard_map/sd,jdc->jsc/dot_general | solution.py:221
  330.4 5.2 %fusion.33.u_q = bf16[416,512]{1,0:T(8,128)(2,1)S(1)} fusion(bf16[3,4096,512]{2,1,0:T(8,128)(2,1)} %all-gather.5.cloned.1.call-done, bf16[544,4096]{1,0:T(8,128)(2,1)} %constant_dynamic-update-slice_fusion.5), kind=kOutput, calls=%fused_computation.30 | convolution fusion | flops 1745043456 | bytes 8028160 | tf_op jit(solution)/shard_map/dot_general | solution.py:220
  335.6 3.4 copy-done.3
  339.0 3.4 copy-done.5
  342.3 7.1 %shard_map.78 = (bf16[256,512]{1,0:T(8,128)(2,1)S(1)}, bf16[3,256,512]{2,1,0:T(8,128)(2,1)S(1)}) custom-call(bf16[416,512]{1,0:T(8,128)(2,1)S(1)} %fusion.33.u_q, bf16[2,416,512]{2,1,0:T(8,128)(2,1)S(1)} %fusion.30.u_kv, bf16[400,2048]{1,0:T(8,128)(2,1)S(1)} %constant_dynamic-update-slice_fusion.3.grad, f32[3,8,2048]{2,1,0:T(8,128)S(1)} %pad.5.filters, ...), custom_call_target="tpu_custom_call" | custom-call | flops 1073741824 | bytes 5242880 | tf_op jit(solution)/shard_map/pallas_call | solution.py:119
  349.5 0.7 copy-done.12
  350.2 13.7 %fusion.12 = bf16[256,4096]{1,0:T(8,128)(2,1)S(1)} fusion(f32[256,4096]{1,0:T(8,128)} %convolution_bitcast_fusion.1, bf16[3,256,512]{2,1,0:T(8,128)(2,1)S(1)} %get-tuple-element.13, bf16[3,4096,512]{2,1,0:T(8,128)(2,1)} %all-gather.5.cloned.1.call-done), kind=kOutput, calls=%fused_computation.17 | convolution fusion | flops 3223322624 | bytes 19660800 | tf_op jit(solution)/shard_map/jsc,jdc->sd/dot_general | solution.py:228
  363.9 1.0 constant_dynamic-slice_fusion
  364.9 1.5 collective-permute-start.6
  366.4 1.1 pad_maximum_fusion
  367.5 23.1 %collective-permute-done.6 = bf16[256,2048]{1,0:T(8,128)(2,1)} collective-permute-done((bf16[256,2048]{1,0:T(8,128)(2,1)}, bf16[256,2048]{1,0:T(8,128)(2,1)}, u32[]{:S(2)}, u32[]{:S(2)}) %collective-permute-start.6) | collective-permute-done | bytes 1048608 | tf_op jit(solution)/shard_map/ppermute | solution.py:22
  390.6 2.6 add_convert_fusion
  (43 shorter events, 0.2 us)
Async XLA Ops:
  7.2 18.5 %copy-start = (bf16[128,128]{1,0:T(8,128)(2,1)S(1)}, bf16[128,128]{1,0:T(8,128)(2,1)}, u32[]{:S(2)}) copy-start(bf16[128,128]{1,0:T(8,128)(2,1)} %param.9) | copy-start | bytes 98308
  7.2 5.6 %copy-start.15 = (bf16[256,2048]{1,0:T(8,128)(2,1)S(1)}, bf16[256,2048]{1,0:T(8,128)(2,1)}, u32[]{:S(2)}) copy-start(bf16[256,2048]{1,0:T(8,128)(2,1)} %param.6) | copy-start | bytes 3145732
  7.2 207.2 %all-gather.3.cloned.1.call-start = ((), (), s32[]{:S(2)}) async-start(), calls=%async_computation | async-start | bytes 40108032 | tf_op jit(solution)/shard_map/all_gather | solution.py:174
  10.5 6.1 %copy-start.18 = (s32[256]{0:T(256)S(1)}, s32[256]{0:T(256)}, u32[]{:S(2)}) copy-start(s32[256]{0:T(256)} %param.10) | copy-start | bytes 3076
  10.5 12.6 %copy-start.16 = (bf16[256,2048]{1,0:T(8,128)(2,1)S(1)}, bf16[256,2048]{1,0:T(8,128)(2,1)}, u32[]{:S(2)}) copy-start(bf16[256,2048]{1,0:T(8,128)(2,1)} %param.11) | copy-start | bytes 3145732
  10.5 311.7 %all-gather.5.cloned.1.call-start = ((), (), s32[]{:S(2)}) async-start(), calls=%async_computation.1 | async-start | bytes 13369344 | tf_op jit(solution)/shard_map/all_gather | solution.py:174
  12.9 17.5 %collective-permute-start = (bf16[144,2048]{1,0:T(8,128)(2,1)S(1)}, bf16[144,2048]{1,0:T(8,128)(2,1)S(1)}, u32[]{:S(2)}, u32[]{:S(2)}) collective-permute-start(bf16[144,2048]{1,0:T(8,128)(2,1)S(1)} %get-tuple-element.15), channel_id=1, source_target_pairs={{0,2},{2,4},{4,6},{6,8},{8,10},{10,12},{12,14},{14,16},{16,18},{18... | collective-permute-start | bytes 1769480 | tf_op jit(solution)/shard_map/ppermute | solution.py:17
  15.3 17.0 %collective-permute-start.1 = (bf16[144,2048]{1,0:T(8,128)(2,1)S(1)}, bf16[144,2048]{1,0:T(8,128)(2,1)S(1)}, u32[]{:S(2)}, u32[]{:S(2)}) collective-permute-start(bf16[144,2048]{1,0:T(8,128)(2,1)S(1)} %get-tuple-element.14), channel_id=1, source_target_pairs={{2,0},{4,2},{6,4},{8,6},{10,8},{12,10},{14,12},{16,14},{18,16},{20... | collective-permute-start | bytes 1769480 | tf_op jit(solution)/shard_map/ppermute | solution.py:17
  16.7 49.8 %collective-permute-start.4 = (s32[144]{0:T(256)S(1)}, s32[144]{0:T(256)S(1)}, u32[]{:S(2)}, u32[]{:S(2)}) collective-permute-start(s32[144]{0:T(256)S(1)} %get-tuple-element.27), channel_id=1, source_target_pairs={{0,2},{2,4},{4,6},{6,8},{8,10},{10,12},{12,14},{14,16},{16,18},{18... | collective-permute-start | bytes 1736 | tf_op jit(solution)/shard_map/ppermute | solution.py:17
  21.8 44.7 %collective-permute-start.5 = (s32[144]{0:T(256)S(1)}, s32[144]{0:T(256)S(1)}, u32[]{:S(2)}, u32[]{:S(2)}) collective-permute-start(s32[144]{0:T(256)S(1)} %get-tuple-element.28), channel_id=1, source_target_pairs={{2,0},{4,2},{6,4},{8,6},{10,8},{12,10},{14,12},{16,14},{18,16},{20... | collective-permute-start | bytes 1736 | tf_op jit(solution)/shard_map/ppermute | solution.py:17
  24.0 43.8 %collective-permute-start.3 = (bf16[144,2048]{1,0:T(8,128)(2,1)}, bf16[144,2048]{1,0:T(8,128)(2,1)}, u32[]{:S(2)}, u32[]{:S(2)}) collective-permute-start(bf16[144,2048]{1,0:T(8,128)(2,1)} %slice.111), channel_id=1, source_target_pairs={{2,0},{4,2},{6,4},{8,6},{10,8},{12,10},{14,12},{16,14},{18,16},{20... | collective-permute-start | bytes 1769480 | tf_op jit(solution)/shard_map/ppermute | solution.py:17
  33.1 43.0 %collective-permute-start.2 = (bf16[544,2048]{1,0:T(8,128)(2,1)}, bf16[544,2048]{1,0:T(8,128)(2,1)}, u32[]{:S(2)}, u32[]{:S(2)}) collective-permute-start(bf16[544,2048]{1,0:T(8,128)(2,1)} %constant_dynamic-update-slice_fusion), channel_id=1, source_target_pairs={{0,1},{1,0},{2,3},{3,2},{4,5},{5,4},{6,7},{7,6},{8,9},{9,8},{10,11... | collective-permute-start | bytes 6684680 | tf_op jit(solution)/shard_map/ppermute | solution.py:22
  52.2 13.0 %copy-start.17 = (f32[3,128,7]{1,2,0:T(8,128)S(1)}, f32[3,128,7]{1,2,0:T(8,128)}, u32[]{:S(2)}) copy-start(f32[3,128,7]{1,2,0:T(8,128)} %param.8) | copy-start | bytes 32260
  223.8 17.0 %copy-start.6 = (bf16[272,256]{1,0:T(8,128)(2,1)S(1)}, bf16[272,256]{1,0:T(8,128)(2,1)}, u32[]{:S(2)}) copy-start(bf16[272,256]{1,0:T(8,128)(2,1)} %get-tuple-element.34.m_bwd) | copy-start | bytes 417796
  240.6 28.4 %copy-start.8 = (s32[256,128]{1,0:T(8,128)}, s32[256,128]{1,0:T(8,128)S(1)}, u32[]{:S(2)}) copy-start(s32[256,128]{1,0:T(8,128)S(1)} %broadcast_in_dim.11.ahead) | copy-start | bytes 393220
  240.8 3.4 copy-start.2
  244.2 3.4 copy-start.4
  269.0 0.9 copy-start.10
  269.9 1.4 copy-start.14
  330.4 5.2 %copy-start.7 = (bf16[272,256]{1,0:T(8,128)(2,1)S(1)}, bf16[272,256]{1,0:T(8,128)(2,1)}, u32[]{:S(2)}) copy-start(bf16[272,256]{1,0:T(8,128)(2,1)} %get-tuple-element.34.m_bwd) | copy-start | bytes 417796
  330.4 5.2 %copy-start.9 = (s32[256,128]{1,0:T(8,128)S(1)}, s32[256,128]{1,0:T(8,128)}, u32[]{:S(2)}) copy-start(s32[256,128]{1,0:T(8,128)} %copy-done.8) | copy-start | bytes 393220
  335.6 3.4 copy-start.3
  339.0 3.4 copy-start.5
  349.5 0.7 copy-start.12
  350.2 16.2 %copy-start.11 = (bf16[256,1536]{1,0:T(8,128)(2,1)S(1)}, bf16[256,1536]{1,0:T(8,128)(2,1)}, u32[]{:S(2)}) copy-start(bf16[256,1536]{1,0:T(8,128)(2,1)} %copy-done.10) | copy-start | bytes 2359300
  350.2 16.2 %copy-start.13 = (bf16[256,512]{1,0:T(8,128)(2,1)S(1)}, bf16[256,512]{1,0:T(8,128)(2,1)}, u32[]{:S(2)}) copy-start(bf16[256,512]{1,0:T(8,128)(2,1)} %copy-done.12) | copy-start | bytes 786436
  350.2 43.0 %copy-start.1 = (bf16[128,128]{1,0:T(8,128)(2,1)S(1)}, bf16[128,128]{1,0:T(8,128)(2,1)}, u32[]{:S(2)}) copy-start(bf16[128,128]{1,0:T(8,128)(2,1)} %param.9) | copy-start | bytes 98308
  364.9 25.7 %collective-permute-start.6 = (bf16[256,2048]{1,0:T(8,128)(2,1)}, bf16[256,2048]{1,0:T(8,128)(2,1)}, u32[]{:S(2)}, u32[]{:S(2)}) collective-permute-start(bf16[256,2048]{1,0:T(8,128)(2,1)} %constant_dynamic-slice_fusion), channel_id=1, source_target_pairs={{0,1},{1,0},{2,3},{3,2},{4,5},{5,4},{6,7},{7,6},{8,9},{9,8},{10,11... | collective-permute-start | bytes 3145736 | tf_op jit(solution)/shard_map/ppermute | solution.py:22
Sparse Core Ops, SparseCore 0:
  10.7 203.6 all-gather.2
  217.1 105.0 all-gather.4

commit v3 on v2

--- a/solution.py
+++ b/solution.py
@@ -146,7 +146,7 @@
             pltpu.VMEM((padded, LANES), jnp.bfloat16),
             pltpu.VMEM((3, near, LANES), jnp.float32),
         ],
-        compiler_params=pltpu.CompilerParams(vmem_limit_bytes=24 * 1024 * 1024),
+        compiler_params=pltpu.CompilerParams(vmem_limit_bytes=57 * 1024 * 1024),
         cost_estimate=pl.CostEstimate(
             flops=width * rows * taps * 64, bytes_accessed=width * rows * 40, transcendentals=0
         ),
@@ -154,7 +154,7 @@
 
 
 def chunk_sizes(width):
-    last = max(1, width // LANES // 4) * LANES
+    last = max(1, width // LANES * 3 // 16) * LANES
     return [size for size in (width - last, last) if size > 0]
 
 

time: 401 us -> 382 us (0.953)
  local copies, waits for them, and re-layouts: 65.1 us -> 49.9 us
  waiting for transfers between devices: 191 us -> 180 us
    unnamed x45 -> x23, local copies, waits for them, and re-layouts: 18.7 us -> 2.23 us
    all_gather x2, waiting for transfers between devices: 167 us -> 158 us  [shards(): weights.append(lax.all_gather(part, 'fsdp', axis=1, tiled=True))]
  transfers between devices with their start and end apart: 9 -> 9, of which waited for: 4 -> 4; matrix products, arithmetic and copies ran while one was open for 25% -> 30% of each run, Pallas kernels for 5% -> 6%
where the time goes in v3:
time: 382 us; the launch traced here: 381 us
  waiting for transfers between devices  180 us (47%)
  matrix products  84.6 us (22%)
  local copies, waits for them, and re-layouts  49.9 us (13%)
  Pallas kernels  31.6 us (8%)
  starting transfers between devices  14.5 us (4%)
  between operations  14.3 us (4%)
  other arithmetic  6.07 us (2%)
    all_gather x2, waiting for transfers between devices, shards(): weights.append(lax.all_gather(part, 'fsdp', axis=1, tiled=True))  158 us
    pallas_call x2, Pallas kernels, convolve(): pl.pallas_call(functools.partial(conv_kernel, rows, taps, short), grid=(w...  31.6 us
    dot_general x2, matrix products, shards(): jnp.einsum('jsc,jdc->sd', grad_u, w, preferred_element_type=jnp.float32)  29.5 us
    dot_general x2, matrix products, shards(): jnp.einsum('sd,jdc->jsc', tokens_kv, w[1:], preferred_element_type=jnp.fl...  27.6 us
    reshape x2, local copies, waits for them, and re-layouts, toeplitz(): table.astype(long_filter.dtype)  25.6 us
    ppermute x2, waiting for transfers between devices, rotated(): lax.ppermute(value, axis, [(at, (at + steps) % count) for at in range(cou...  22.5 us
    dot_general x2, matrix products, shards(): jnp.dot(tokens_q, w[0], preferred_element_type=jnp.float32)  18.4 us
    ppermute x5, starting transfers between devices, shifted(): lax.ppermute(value, axis, [(at, at + steps) for at in range(first, last)])  11.4 us
  transfers between devices with their start and end apart: 9, of which 4 were waited for; matrix products, arithmetic and copies ran while one was open for 30% of the time, Pallas kernels for 6%

profile of v3, /device:TPU:0, one launch (start us, length us, event | category | flops | bytes accessed | tf_op | source)
XLA Modules:
  0.0 381.3 jit_solution(10609887567430360458)
XLA Ops:
  7.2 0.0 copy-start
  7.2 0.0 all-gather.3.cloned.1.call-start
  7.2 3.4 slice.107
  10.7 0.0 all-gather.3.cloned.1.call-update
  10.7 0.0 all-gather.5.cloned.1.call-start
  10.8 2.0 slice.134
  12.8 0.0 all-gather.5.cloned.1.call-update
  12.8 0.1 fusion.43
  12.9 2.4 collective-permute-start
  15.3 1.3 collective-permute-start.1
  16.6 0.1 fusion.46
  16.7 5.1 %collective-permute-start.4 = (s32[144]{0:T(256)S(1)}, s32[144]{0:T(256)S(1)}, u32[]{:S(2)}, u32[]{:S(2)}) collective-permute-start(s32[144]{0:T(256)S(1)} %get-tuple-element.27), channel_id=1, source_target_pairs={{0,2},{2,4},{4,6},{6,8},{8,10},{10,12},{12,14},{14,16},{16,18},{18... | collective-permute-start | bytes 1736 | tf_op jit(solution)/shard_map/ppermute | solution.py:17
  21.8 1.3 collective-permute-start.5
  23.2 0.9 slice.111
  24.0 1.3 collective-permute-start.3
  25.3 0.1 copy.14
  25.4 0.1 copy.15
  25.5 0.2 iota.51
  25.7 4.6 %convolution_convert_fusion.1 = bf16[32768,128]{1,0:T(8,128)(2,1)} fusion(bf16[128,128]{1,0:T(8,128)(2,1)S(1)} %copy-done, s32[32768]{0:T(1024)S(1)} %get-tuple-element.17), kind=kOutput, calls=%fused_computation.1 | convolution fusion | flops 1086324736 | bytes 8552448 | tf_op jit(solution)/shard_map/dot_general | solution.py:44
  30.3 0.0 collective-permute-done
  30.3 0.9 constant_dynamic-update-slice_fusion.2
  31.2 1.1 constant_dynamic-update-slice_fusion.1
  32.3 0.9 constant_dynamic-update-slice_fusion
  33.1 1.5 collective-permute-start.2
  34.6 4.6 %convolution_convert_fusion = bf16[32768,128]{1,0:T(8,128)(2,1)} fusion(bf16[128,128]{1,0:T(8,128)(2,1)S(1)} %copy-done, s32[32768]{0:T(1024)S(1)} %get-tuple-element.16), kind=kOutput, calls=%fused_computation | convolution fusion | flops 1086324736 | bytes 8552448 | tf_op jit(solution)/shard_map/dot_general | solution.py:44
  39.2 12.8 %copy.12.t_fwd = bf16[128,128,256]{2,1,0:T(8,128)(2,1)} copy(bf16[128,128,256]{0,2,1:T(8,128)(2,1)} %bitcast.52) | data formatting | bytes 16777216 | tf_op jit(solution)/shard_map/reshape | solution.py:45
  52.1 0.1 constant_dynamic-update-slice_fusion.4
  52.2 0.0 copy-start.6
  52.2 12.8 %copy.13.t_bwd = bf16[128,128,256]{2,1,0:T(8,128)(2,1)} copy(bf16[128,128,256]{0,2,1:T(8,128)(2,1)} %bitcast.53) | data formatting | bytes 16777216 | tf_op jit(solution)/shard_map/reshape | solution.py:45
  65.0 0.4 broadcast_in_dim.9
  65.4 0.8 reshape.51
  66.2 0.7 pad.5.filters
  66.9 0.1 add_add_fusion
  67.0 0.1 slice.118
  67.1 0.1 fusion.42
  67.1 0.1 broadcast_compare_fusion.4
  67.2 0.1 fusion.45
  67.3 0.1 broadcast_compare_fusion.1
  67.4 0.7 add_convert_fusion.1
  68.2 0.1 convert_add_fusion
  68.3 0.0 collective-permute-done.3
  68.3 1.1 constant_dynamic-update-slice_fusion.3.grad
  69.4 2.6 broadcast_in_dim.8
  72.0 3.4 constant_dynamic-update-slice_fusion.6
  75.4 0.8 collective-permute-done.2
  76.1 3.6 constant_dynamic-update-slice_fusion.5
  79.8 149.4 %all-gather.3.cloned.1.call-done = bf16[3,4096,1664]{2,1,0:T(8,128)(2,1)} async-done(((bf16[3,256,1664]{2,1,0:T(8,128)(2,1)}), bf16[3,4096,1664]{2,1,0:T(8,128)(2,1)}) %all-gather.3.cloned.1.call-update) | async-done | bytes 40894480 | tf_op jit(solution)/shard_map/all_gather | solution.py:174
  229.1 12.8 %fusion.24.u_q = bf16[416,1664]{1,0:T(8,128)(2,1)} fusion(bf16[3,4096,1664]{2,1,0:T(8,128)(2,1)} %all-gather.3.cloned.1.call-done, bf16[544,4096]{1,0:T(8,128)(2,1)} %constant_dynamic-update-slice_fusion.5), kind=kOutput, calls=%fused_computation.26 | convolution fusion | flops 5671391232 | bytes 18423808 | tf_op jit(solution)/shard_map/dot_general | solution.py:220
  241.9 20.2 %fusion.19.u_kv = bf16[2,416,1664]{2,1,0:T(8,128)(2,1)} fusion(bf16[3,4096,1664]{2,1,0:T(8,128)(2,1)} %all-gather.3.cloned.1.call-done, bf16[544,4096]{1,0:T(8,128)(2,1)} %constant_dynamic-update-slice_fusion.5), kind=kOutput, calls=%fused_computation.23 | convolution fusion | flops 11342782464 | bytes 33439744 | tf_op jit(solution)/shard_map/sd,jdc->jsc/dot_general | solution.py:221
  262.1 0.8 broadcast_in_dim.11.ahead
  262.9 0.9 broadcast_in_dim.10.back
  263.7 24.2 %shard_map.77 = (bf16[256,1664]{1,0:T(8,128)(2,1)}, bf16[3,256,1664]{2,1,0:T(8,128)(2,1)}) custom-call(bf16[416,1664]{1,0:T(8,128)(2,1)} %fusion.24.u_q, bf16[2,416,1664]{2,1,0:T(8,128)(2,1)} %fusion.19.u_kv, bf16[400,2048]{1,0:T(8,128)(2,1)} %copy-done.2, f32[3,8,2048]{2,1,0:T(8,128)} %pad.5.filters, bf16[128,128,256]{2,1,0:T(8,128)(2,1)} %copy.12.t_fwd, ...), custom_call_target="tpu_custom_call" | custom-call | flops 3489660928 | bytes 17039360 | tf_op jit(solution)/shard_map/pallas_call | solution.py:119
  287.9 21.5 %convolution_bitcast_fusion = f32[256,4096]{1,0:T(8,128)} fusion(bf16[3,256,1664]{2,1,0:T(8,128)(2,1)} %get-tuple-element.9, bf16[3,4096,1664]{2,1,0:T(8,128)(2,1)} %all-gather.3.cloned.1.call-done), kind=kOutput, calls=%fused_computation.14 | convolution fusion | flops 10468982784 | bytes 47644672 | tf_op jit(solution)/shard_map/jsc,jdc->sd/dot_general | solution.py:228
  309.4 8.5 %all-gather.5.cloned.1.call-done = bf16[3,4096,384]{2,1,0:T(8,128)(2,1)} async-done(((bf16[3,256,384]{2,1,0:T(8,128)(2,1)}), bf16[3,4096,384]{2,1,0:T(8,128)(2,1)}) %all-gather.5.cloned.1.call-update) | async-done | bytes 9437200 | tf_op jit(solution)/shard_map/all_gather | solution.py:174
  317.9 7.4 %fusion.30.u_kv = bf16[2,416,384]{2,1,0:T(8,128)(2,1)} fusion(bf16[3,4096,384]{2,1,0:T(8,128)(2,1)} %all-gather.5.cloned.1.call-done, bf16[544,4096]{1,0:T(8,128)(2,1)} %constant_dynamic-update-slice_fusion.5), kind=kOutput, calls=%fused_computation.29 | convolution fusion | flops 2617565184 | bytes 10338304 | tf_op jit(solution)/shard_map/sd,jdc->jsc/dot_general | solution.py:221
  325.3 5.6 %fusion.33.u_q = bf16[416,384]{1,0:T(8,128)(2,1)} fusion(bf16[3,4096,384]{2,1,0:T(8,128)(2,1)} %all-gather.5.cloned.1.call-done, bf16[544,4096]{1,0:T(8,128)(2,1)} %constant_dynamic-update-slice_fusion.5), kind=kOutput, calls=%fused_computation.30 | convolution fusion | flops 1308782592 | bytes 6873088 | tf_op jit(solution)/shard_map/dot_general | solution.py:220
  330.9 7.3 %shard_map.78 = (bf16[256,384]{1,0:T(8,128)(2,1)}, bf16[3,256,384]{2,1,0:T(8,128)(2,1)}) custom-call(bf16[416,384]{1,0:T(8,128)(2,1)} %fusion.33.u_q, bf16[2,416,384]{2,1,0:T(8,128)(2,1)} %fusion.30.u_kv, bf16[400,2048]{1,0:T(8,128)(2,1)} %copy-done.2, f32[3,8,2048]{2,1,0:T(8,128)} %pad.5.filters, bf16[128,128,256]{2,1,0:T(8,128)(2,1)} %copy.12.t_fwd, ...), custom_call_target="tpu_custom_call" | custom-call | flops 805306368 | bytes 3932160 | tf_op jit(solution)/shard_map/pallas_call | solution.py:119
  338.3 0.0 copy-start.1
  338.3 8.0 %fusion.12 = bf16[256,4096]{1,0:T(8,128)(2,1)S(1)} fusion(f32[256,4096]{1,0:T(8,128)} %convolution_bitcast_fusion, bf16[3,256,384]{2,1,0:T(8,128)(2,1)} %get-tuple-element.13, bf16[3,4096,384]{2,1,0:T(8,128)(2,1)} %all-gather.5.cloned.1.call-done), kind=kOutput, calls=%fused_computation.17 | convolution fusion | flops 2418016256 | bytes 16318464 | tf_op jit(solution)/shard_map/jsc,jdc->sd/dot_general | solution.py:228
  346.3 0.1 constant_dynamic-slice_fusion
  346.4 1.5 collective-permute-start.6
  347.9 2.3 pad_maximum_fusion
  350.2 21.7 %collective-permute-done.6 = bf16[256,2048]{1,0:T(8,128)(2,1)} collective-permute-done((bf16[256,2048]{1,0:T(8,128)(2,1)S(1)}, bf16[256,2048]{1,0:T(8,128)(2,1)}, u32[]{:S(2)}, u32[]{:S(2)}) %collective-permute-start.6) | collective-permute-done | bytes 1048608 | tf_op jit(solution)/shard_map/ppermute | solution.py:22
  371.9 2.6 add_convert_fusion
  (21 shorter events, 0.1 us)
Async XLA Ops:
  7.2 18.6 %copy-start = (bf16[128,128]{1,0:T(8,128)(2,1)S(1)}, bf16[128,128]{1,0:T(8,128)(2,1)}, u32[]{:S(2)}) copy-start(bf16[128,128]{1,0:T(8,128)(2,1)} %param.9) | copy-start | bytes 98308
  7.2 5.6 %copy-start.3 = (bf16[256,2048]{1,0:T(8,128)(2,1)S(1)}, bf16[256,2048]{1,0:T(8,128)(2,1)}, u32[]{:S(2)}) copy-start(bf16[256,2048]{1,0:T(8,128)(2,1)} %param.6) | copy-start | bytes 3145732
  7.2 221.9 %all-gather.3.cloned.1.call-start = ((), (), s32[]{:S(2)}) async-start(), calls=%async_computation | async-start | bytes 43450368 | tf_op jit(solution)/shard_map/all_gather | solution.py:174
  10.7 5.9 %copy-start.7 = (s32[256]{0:T(256)S(1)}, s32[256]{0:T(256)}, u32[]{:S(2)}) copy-start(s32[256]{0:T(256)} %param.10) | copy-start | bytes 3076
  10.7 12.5 %copy-start.4 = (bf16[256,2048]{1,0:T(8,128)(2,1)S(1)}, bf16[256,2048]{1,0:T(8,128)(2,1)}, u32[]{:S(2)}) copy-start(bf16[256,2048]{1,0:T(8,128)(2,1)} %param.11) | copy-start | bytes 3145732
  10.7 307.2 %all-gather.5.cloned.1.call-start = ((), (), s32[]{:S(2)}) async-start(), calls=%async_computation.1 | async-start | bytes 10027008 | tf_op jit(solution)/shard_map/all_gather | solution.py:174
  12.9 17.4 %collective-permute-start = (bf16[144,2048]{1,0:T(8,128)(2,1)S(1)}, bf16[144,2048]{1,0:T(8,128)(2,1)S(1)}, u32[]{:S(2)}, u32[]{:S(2)}) collective-permute-start(bf16[144,2048]{1,0:T(8,128)(2,1)S(1)} %get-tuple-element.15), channel_id=1, source_target_pairs={{0,2},{2,4},{4,6},{6,8},{8,10},{10,12},{12,14},{14,16},{16,18},{18... | collective-permute-start | bytes 1769480 | tf_op jit(solution)/shard_map/ppermute | solution.py:17
  15.3 16.9 %collective-permute-start.1 = (bf16[144,2048]{1,0:T(8,128)(2,1)S(1)}, bf16[144,2048]{1,0:T(8,128)(2,1)S(1)}, u32[]{:S(2)}, u32[]{:S(2)}) collective-permute-start(bf16[144,2048]{1,0:T(8,128)(2,1)S(1)} %get-tuple-element.14), channel_id=1, source_target_pairs={{2,0},{4,2},{6,4},{8,6},{10,8},{12,10},{14,12},{16,14},{18,16},{20... | collective-permute-start | bytes 1769480 | tf_op jit(solution)/shard_map/ppermute | solution.py:17
  16.7 50.2 %collective-permute-start.4 = (s32[144]{0:T(256)S(1)}, s32[144]{0:T(256)S(1)}, u32[]{:S(2)}, u32[]{:S(2)}) collective-permute-start(s32[144]{0:T(256)S(1)} %get-tuple-element.27), channel_id=1, source_target_pairs={{0,2},{2,4},{4,6},{6,8},{8,10},{10,12},{12,14},{14,16},{16,18},{18... | collective-permute-start | bytes 1736 | tf_op jit(solution)/shard_map/ppermute | solution.py:17
  21.8 45.1 %collective-permute-start.5 = (s32[144]{0:T(256)S(1)}, s32[144]{0:T(256)S(1)}, u32[]{:S(2)}, u32[]{:S(2)}) collective-permute-start(s32[144]{0:T(256)S(1)} %get-tuple-element.28), channel_id=1, source_target_pairs={{2,0},{4,2},{6,4},{8,6},{10,8},{12,10},{14,12},{16,14},{18,16},{20... | collective-permute-start | bytes 1736 | tf_op jit(solution)/shard_map/ppermute | solution.py:17
  24.0 44.3 %collective-permute-start.3 = (bf16[144,2048]{1,0:T(8,128)(2,1)}, bf16[144,2048]{1,0:T(8,128)(2,1)}, u32[]{:S(2)}, u32[]{:S(2)}) collective-permute-start(bf16[144,2048]{1,0:T(8,128)(2,1)} %slice.111), channel_id=1, source_target_pairs={{2,0},{4,2},{6,4},{8,6},{10,8},{12,10},{14,12},{16,14},{18,16},{20... | collective-permute-start | bytes 1769480 | tf_op jit(solution)/shard_map/ppermute | solution.py:17
  33.1 43.0 %collective-permute-start.2 = (bf16[544,2048]{1,0:T(8,128)(2,1)}, bf16[544,2048]{1,0:T(8,128)(2,1)}, u32[]{:S(2)}, u32[]{:S(2)}) collective-permute-start(bf16[544,2048]{1,0:T(8,128)(2,1)} %constant_dynamic-update-slice_fusion), channel_id=1, source_target_pairs={{0,1},{1,0},{2,3},{3,2},{4,5},{5,4},{6,7},{7,6},{8,9},{9,8},{10,11... | collective-permute-start | bytes 6684680 | tf_op jit(solution)/shard_map/ppermute | solution.py:22
  52.2 12.8 %copy-start.6 = (f32[3,128,7]{1,2,0:T(8,128)S(1)}, f32[3,128,7]{1,2,0:T(8,128)}, u32[]{:S(2)}) copy-start(f32[3,128,7]{1,2,0:T(8,128)} %param.8) | copy-start | bytes 32260
  69.4 6.0 %copy-start.2 = (bf16[400,2048]{1,0:T(8,128)(2,1)}, bf16[400,2048]{1,0:T(8,128)(2,1)S(1)}, u32[]{:S(2)}) copy-start(bf16[400,2048]{1,0:T(8,128)(2,1)S(1)} %constant_dynamic-update-slice_fusion.3.grad) | copy-start | bytes 4915204
  338.3 9.7 %copy-start.5 = (bf16[256,384]{1,0:T(8,128)(2,1)S(1)}, bf16[256,384]{1,0:T(8,128)(2,1)}, u32[]{:S(2)}) copy-start(bf16[256,384]{1,0:T(8,128)(2,1)} %get-tuple-element.11) | copy-start | bytes 589828
  338.3 36.2 %copy-start.1 = (bf16[128,128]{1,0:T(8,128)(2,1)S(1)}, bf16[128,128]{1,0:T(8,128)(2,1)}, u32[]{:S(2)}) copy-start(bf16[128,128]{1,0:T(8,128)(2,1)} %param.9) | copy-start | bytes 98308
  346.4 25.5 %collective-permute-start.6 = (bf16[256,2048]{1,0:T(8,128)(2,1)S(1)}, bf16[256,2048]{1,0:T(8,128)(2,1)}, u32[]{:S(2)}, u32[]{:S(2)}) collective-permute-start(bf16[256,2048]{1,0:T(8,128)(2,1)S(1)} %constant_dynamic-slice_fusion), channel_id=1, source_target_pairs={{0,1},{1,0},{2,3},{3,2},{4,5},{5,4},{6,7},{7,6},{8,9},{9,8},{10,11... | collective-permute-start | bytes 3145736 | tf_op jit(solution)/shard_map/ppermute | solution.py:22
Sparse Core Ops, SparseCore 0:
  10.8 218.2 all-gather.2
  232.0 85.8 all-gather.4

commit v4 on v3

--- a/solution.py
+++ b/solution.py
@@ -158,6 +158,10 @@
     return [size for size in (width - last, last) if size > 0]
 
 
+def backward(grad_u, w):
+    return jnp.einsum("jsc,jdc->sd", grad_u, w, preferred_element_type=jnp.float32)
+
+
 def shards(tokens, w_feat, short_filter, long_filter, doc_ids, grad_out):
     rows = tokens.shape[0]
     taps = long_filter.shape[1]
@@ -225,20 +229,28 @@
             rows, taps, short, start, u_q, u_kv, grad_ext, filters, t_fwd, t_bwd, m_fwd, m_bwd, back, ahead
         )
         mixed.append(part)
-        term = jnp.einsum("jsc,jdc->sd", grad_u, w, preferred_element_type=jnp.float32)
-        partial = term if partial is None else partial + term
+        if start + size < channels:
+            term = backward(grad_u, w)
+            partial = term if partial is None else partial + term
         start += size
     mixed = jnp.concatenate(mixed, axis=1)
 
-    partial = partial.astype(jnp.bfloat16)
     width = tokens.shape[1]
     here = lax.axis_index("tp")
-    total = lax.dynamic_slice(partial, (0, here * width), (rows, width)).astype(jnp.float32)
-    for step in range(1, tp):
-        to = (here + step) % tp
-        block = lax.dynamic_slice(partial, (0, to * width), (rows, width))
-        total = total + rotated(block, "tp", step).astype(jnp.float32)
-    return mixed, total.astype(jnp.bfloat16)
+    half = rows // 2
+    outs = []
+    for at in (0, half):
+        term = backward(grad_u[:, at : at + half], w)
+        if partial is not None:
+            term = partial[at : at + half] + term
+        term = term.astype(jnp.bfloat16)
+        total = lax.dynamic_slice(term, (0, here * width), (half, width)).astype(jnp.float32)
+        for step in range(1, tp):
+            to = (here + step) % tp
+            block = lax.dynamic_slice(term, (0, to * width), (half, width))
+            total = total + rotated(block, "tp", step).astype(jnp.float32)
+        outs.append(total.astype(jnp.bfloat16))
+    return mixed, jnp.concatenate(outs, axis=0)
 
 
 def solution(mesh):

time: 382 us -> 381 us (level)
    dot_general x2 -> x3, matrix products: 29.5 us -> 32.2 us  [backward(): jnp.einsum('jsc,jdc->sd', grad_u, w, preferred_element_type=jnp.float32)]
    ppermute x2 -> x3, waiting for transfers between devices: 22.5 us -> 19.8 us  [rotated(): lax.ppermute(value, axis, [(at, (at + steps) % count) for at in range(cou...]
  transfers between devices with their start and end apart: 9 -> 10, of which waited for: 4 -> 5; matrix products, arithmetic and copies ran while one was open for 30% -> 30% of each run, Pallas kernels for 6% -> 6%
where the time goes in v4:
time: 381 us; the launch traced here: 380 us
  waiting for transfers between devices  178 us (47%)
  matrix products  87.5 us (23%)
  local copies, waits for them, and re-layouts  49.5 us (13%)
  Pallas kernels  31.7 us (8%)
  starting transfers between devices  15.1 us (4%)
  between operations  14.4 us (4%)
    all_gather x2, waiting for transfers between devices, shards(): weights.append(lax.all_gather(part, 'fsdp', axis=1, tiled=True))  158 us
    dot_general x3, matrix products, backward(): jnp.einsum('jsc,jdc->sd', grad_u, w, preferred_element_type=jnp.float32)  32.2 us
    pallas_call x2, Pallas kernels, convolve(): pl.pallas_call(functools.partial(conv_kernel, rows, taps, short), grid=(w...  31.7 us
    dot_general x2, matrix products, shards(): jnp.einsum('sd,jdc->jsc', tokens_kv, w[1:], preferred_element_type=jnp.fl...  27.6 us
    reshape x2, local copies, waits for them, and re-layouts, toeplitz(): table.astype(long_filter.dtype)  25.3 us
    ppermute x3, waiting for transfers between devices, rotated(): lax.ppermute(value, axis, [(at, (at + steps) % count) for at in range(cou...  19.8 us
    dot_general x2, matrix products, shards(): jnp.dot(tokens_q, w[0], preferred_element_type=jnp.float32)  18.4 us
    ppermute x5, starting transfers between devices, shifted(): lax.ppermute(value, axis, [(at, at + steps) for at in range(first, last)])  11.4 us
  transfers between devices with their start and end apart: 10, of which 5 were waited for; matrix products, arithmetic and copies ran while one was open for 30% of the time, Pallas kernels for 6%

profile of v4, /device:TPU:0, one launch (start us, length us, event | category | flops | bytes accessed | tf_op | source)
XLA Modules:
  0.0 379.6 jit_solution(12258062975346494134)
XLA Ops:
  7.2 0.0 copy-start
  7.2 0.0 all-gather.3.cloned.1.call-start
  7.2 3.4 slice.119
  10.7 0.0 all-gather.3.cloned.1.call-update
  10.7 0.0 all-gather.5.cloned.1.call-start
  10.7 2.0 slice.146
  12.8 0.0 all-gather.5.cloned.1.call-update
  12.8 0.1 fusion.47
  12.9 2.4 collective-permute-start
  15.3 1.3 collective-permute-start.1
  16.6 0.1 fusion.50
  16.7 5.1 %collective-permute-start.4 = (s32[144]{0:T(256)S(1)}, s32[144]{0:T(256)S(1)}, u32[]{:S(2)}, u32[]{:S(2)}) collective-permute-start(s32[144]{0:T(256)S(1)} %get-tuple-element.27), channel_id=1, source_target_pairs={{0,2},{2,4},{4,6},{6,8},{8,10},{10,12},{12,14},{14,16},{16,18},{18... | collective-permute-start | bytes 1736 | tf_op jit(solution)/shard_map/ppermute | solution.py:17
  21.8 1.3 collective-permute-start.5
  23.1 0.9 slice.123
  24.0 1.3 collective-permute-start.3
  25.3 0.1 copy.14
  25.4 0.1 copy.15
  25.5 0.2 iota.51
  25.7 4.6 %convolution_convert_fusion.1 = bf16[32768,128]{1,0:T(8,128)(2,1)} fusion(bf16[128,128]{1,0:T(8,128)(2,1)S(1)} %copy-done, s32[32768]{0:T(1024)S(1)} %get-tuple-element.17), kind=kOutput, calls=%fused_computation.1 | convolution fusion | flops 1086324736 | bytes 8552448 | tf_op jit(solution)/shard_map/dot_general | solution.py:44
  30.4 0.9 constant_dynamic-update-slice_fusion.2
  31.2 1.0 constant_dynamic-update-slice_fusion.1
  32.3 0.9 constant_dynamic-update-slice_fusion
  33.2 1.5 collective-permute-start.2
  34.7 4.6 %convolution_convert_fusion = bf16[32768,128]{1,0:T(8,128)(2,1)} fusion(bf16[128,128]{1,0:T(8,128)(2,1)S(1)} %copy-done, s32[32768]{0:T(1024)S(1)} %get-tuple-element.16), kind=kOutput, calls=%fused_computation | convolution fusion | flops 1086324736 | bytes 8552448 | tf_op jit(solution)/shard_map/dot_general | solution.py:44
  39.3 13.0 %copy.12.t_fwd = bf16[128,128,256]{2,1,0:T(8,128)(2,1)} copy(bf16[128,128,256]{0,2,1:T(8,128)(2,1)} %bitcast.60) | data formatting | bytes 16777216 | tf_op jit(solution)/shard_map/reshape | solution.py:45
  52.3 0.1 constant_dynamic-update-slice_fusion.4
  52.4 12.3 %copy.13.t_bwd = bf16[128,128,256]{2,1,0:T(8,128)(2,1)} copy(bf16[128,128,256]{0,2,1:T(8,128)(2,1)} %bitcast.61) | data formatting | bytes 16777216 | tf_op jit(solution)/shard_map/reshape | solution.py:45
  64.6 0.4 broadcast_in_dim.9
  65.1 0.8 reshape.51
  65.9 0.7 pad.5.filters
  66.6 0.1 add_add_fusion
  66.6 0.1 slice.130
  66.7 0.1 fusion.46
  66.8 0.1 broadcast_compare_fusion.4
  66.9 0.1 fusion.49
  66.9 0.1 broadcast_compare_fusion.1
  67.1 0.7 add_convert_fusion.2
  67.8 0.1 convert_add_fusion
  67.9 1.1 constant_dynamic-update-slice_fusion.3.grad
  69.0 2.6 broadcast_in_dim.8
  71.7 3.4 constant_dynamic-update-slice_fusion.6
  75.1 1.1 collective-permute-done.2
  76.2 3.6 constant_dynamic-update-slice_fusion.5
  79.8 149.4 %all-gather.3.cloned.1.call-done = bf16[3,4096,1664]{2,1,0:T(8,128)(2,1)} async-done(((bf16[3,256,1664]{2,1,0:T(8,128)(2,1)}), bf16[3,4096,1664]{2,1,0:T(8,128)(2,1)}) %all-gather.3.cloned.1.call-update) | async-done | bytes 40894480 | tf_op jit(solution)/shard_map/all_gather | solution.py:178
  229.1 12.9 %fusion.26.u_q = bf16[416,1664]{1,0:T(8,128)(2,1)} fusion(bf16[3,4096,1664]{2,1,0:T(8,128)(2,1)} %all-gather.3.cloned.1.call-done, bf16[544,4096]{1,0:T(8,128)(2,1)} %constant_dynamic-update-slice_fusion.5), kind=kOutput, calls=%fused_computation.29 | convolution fusion | flops 5671391232 | bytes 18423808 | tf_op jit(solution)/shard_map/dot_general | solution.py:224
  242.0 20.2 %fusion.21.u_kv = bf16[2,416,1664]{2,1,0:T(8,128)(2,1)} fusion(bf16[3,4096,1664]{2,1,0:T(8,128)(2,1)} %all-gather.3.cloned.1.call-done, bf16[544,4096]{1,0:T(8,128)(2,1)} %constant_dynamic-update-slice_fusion.5), kind=kOutput, calls=%fused_computation.26 | convolution fusion | flops 11342782464 | bytes 33439744 | tf_op jit(solution)/shard_map/sd,jdc->jsc/dot_general | solution.py:225
  262.1 0.8 broadcast_in_dim.11.ahead
  262.9 0.8 broadcast_in_dim.10.back
  263.7 24.2 %shard_map.77 = (bf16[256,1664]{1,0:T(8,128)(2,1)}, bf16[3,256,1664]{2,1,0:T(8,128)(2,1)}) custom-call(bf16[416,1664]{1,0:T(8,128)(2,1)} %fusion.26.u_q, bf16[2,416,1664]{2,1,0:T(8,128)(2,1)} %fusion.21.u_kv, bf16[400,2048]{1,0:T(8,128)(2,1)} %copy-done.2, f32[3,8,2048]{2,1,0:T(8,128)} %pad.5.filters, bf16[128,128,256]{2,1,0:T(8,128)(2,1)} %copy.12.t_fwd, ...), custom_call_target="tpu_custom_call" | custom-call | flops 3489660928 | bytes 17039360 | tf_op jit(solution)/shard_map/pallas_call | solution.py:119
  287.9 21.5 %convolution_bitcast_fusion = f32[256,4096]{1,0:T(8,128)} fusion(bf16[3,256,1664]{2,1,0:T(8,128)(2,1)} %get-tuple-element.9, bf16[3,4096,1664]{2,1,0:T(8,128)(2,1)} %all-gather.3.cloned.1.call-done), kind=kOutput, calls=%fused_computation.14 | convolution fusion | flops 10468982784 | bytes 47644672 | tf_op jit(solution)/shard_map/jsc,jdc->sd/dot_general | solution.py:162
  309.4 8.5 %all-gather.5.cloned.1.call-done = bf16[3,4096,384]{2,1,0:T(8,128)(2,1)} async-done(((bf16[3,256,384]{2,1,0:T(8,128)(2,1)}), bf16[3,4096,384]{2,1,0:T(8,128)(2,1)}) %all-gather.5.cloned.1.call-update) | async-done | bytes 9437200 | tf_op jit(solution)/shard_map/all_gather | solution.py:178
  317.9 7.4 %fusion.32.u_kv = bf16[2,416,384]{2,1,0:T(8,128)(2,1)} fusion(bf16[3,4096,384]{2,1,0:T(8,128)(2,1)} %all-gather.5.cloned.1.call-done, bf16[544,4096]{1,0:T(8,128)(2,1)} %constant_dynamic-update-slice_fusion.5), kind=kOutput, calls=%fused_computation.31 | convolution fusion | flops 2617565184 | bytes 10338304 | tf_op jit(solution)/shard_map/sd,jdc->jsc/dot_general | solution.py:225
  325.3 5.6 %fusion.35.u_q = bf16[416,384]{1,0:T(8,128)(2,1)} fusion(bf16[3,4096,384]{2,1,0:T(8,128)(2,1)} %all-gather.5.cloned.1.call-done, bf16[544,4096]{1,0:T(8,128)(2,1)} %constant_dynamic-update-slice_fusion.5), kind=kOutput, calls=%fused_computation.32 | convolution fusion | flops 1308782592 | bytes 6873088 | tf_op jit(solution)/shard_map/dot_general | solution.py:224
  330.9 7.5 %shard_map.78 = (bf16[256,384]{1,0:T(8,128)(2,1)}, bf16[3,256,384]{2,1,0:T(8,128)(2,1)}) custom-call(bf16[416,384]{1,0:T(8,128)(2,1)} %fusion.35.u_q, bf16[2,416,384]{2,1,0:T(8,128)(2,1)} %fusion.32.u_kv, bf16[400,2048]{1,0:T(8,128)(2,1)} %copy-done.2, f32[3,8,2048]{2,1,0:T(8,128)} %pad.5.filters, bf16[128,128,256]{2,1,0:T(8,128)(2,1)} %copy.12.t_fwd, ...), custom_call_target="tpu_custom_call" | custom-call | flops 805306368 | bytes 3932160 | tf_op jit(solution)/shard_map/pallas_call | solution.py:119
  338.4 7.6 %fusion.14 = bf16[128,4096]{1,0:T(8,128)(2,1)S(1)} fusion(bf16[3,4096,384]{2,1,0:T(8,128)(2,1)} %all-gather.5.cloned.1.call-done, f32[256,4096]{1,0:T(8,128)} %convolution_bitcast_fusion, bf16[3,256,384]{2,1,0:T(8,128)(2,1)} %get-tuple-element.13), kind=kOutput, calls=%fused_computation.20 | convolution fusion | flops 1209008128 | bytes 12877824 | tf_op jit(solution)/shard_map/jsc,jdc->sd/dot_general | solution.py:162
  346.1 1.5 collective-permute-start.6
  347.7 3.1 fusion.13
  350.9 0.6 collective-permute-start.7
  351.5 1.1 pad_maximum_fusion
  352.6 8.3 %collective-permute-done.6 = bf16[128,2048]{1,0:T(8,128)(2,1)S(1)} collective-permute-done((bf16[128,2048]{1,0:T(8,128)(2,1)S(1)}, bf16[128,2048]{1,0:T(8,128)(2,1)S(1)}, u32[]{:S(2)}, u32[]{:S(2)}) %collective-permute-start.6) | collective-permute-done | bytes 524320 | tf_op jit(solution)/shard_map/ppermute | solution.py:22
  360.9 0.1 add_convert_fusion.1
  361.1 10.4 %collective-permute-done.7 = bf16[128,2048]{1,0:T(8,128)(2,1)S(1)} collective-permute-done((bf16[128,2048]{1,0:T(8,128)(2,1)S(1)}, bf16[128,2048]{1,0:T(8,128)(2,1)S(1)}, u32[]{:S(2)}, u32[]{:S(2)}) %collective-permute-start.7) | collective-permute-done | bytes 524320 | tf_op jit(solution)/shard_map/ppermute | solution.py:22
  371.5 0.1 add_convert_fusion
  371.6 1.1 pad_maximum_fusion.1
  (40 shorter events, 0.2 us)
Async XLA Ops:
  7.2 18.6 %copy-start = (bf16[128,128]{1,0:T(8,128)(2,1)S(1)}, bf16[128,128]{1,0:T(8,128)(2,1)}, u32[]{:S(2)}) copy-start(bf16[128,128]{1,0:T(8,128)(2,1)} %param.9) | copy-start | bytes 98308
  7.2 5.6 %copy-start.3 = (bf16[256,2048]{1,0:T(8,128)(2,1)S(1)}, bf16[256,2048]{1,0:T(8,128)(2,1)}, u32[]{:S(2)}) copy-start(bf16[256,2048]{1,0:T(8,128)(2,1)} %param.6) | copy-start | bytes 3145732
  7.2 221.9 %all-gather.3.cloned.1.call-start = ((), (), s32[]{:S(2)}) async-start(), calls=%async_computation | async-start | bytes 43450368 | tf_op jit(solution)/shard_map/all_gather | solution.py:178
  10.7 5.9 %copy-start.10 = (s32[256]{0:T(256)S(1)}, s32[256]{0:T(256)}, u32[]{:S(2)}) copy-start(s32[256]{0:T(256)} %param.10) | copy-start | bytes 3076
  10.7 12.5 %copy-start.5 = (bf16[256,2048]{1,0:T(8,128)(2,1)S(1)}, bf16[256,2048]{1,0:T(8,128)(2,1)}, u32[]{:S(2)}) copy-start(bf16[256,2048]{1,0:T(8,128)(2,1)} %param.11) | copy-start | bytes 3145732
  10.7 307.2 %all-gather.5.cloned.1.call-start = ((), (), s32[]{:S(2)}) async-start(), calls=%async_computation.1 | async-start | bytes 10027008 | tf_op jit(solution)/shard_map/all_gather | solution.py:178
  12.9 17.5 %collective-permute-start = (bf16[144,2048]{1,0:T(8,128)(2,1)S(1)}, bf16[144,2048]{1,0:T(8,128)(2,1)S(1)}, u32[]{:S(2)}, u32[]{:S(2)}) collective-permute-start(bf16[144,2048]{1,0:T(8,128)(2,1)S(1)} %get-tuple-element.15), channel_id=1, source_target_pairs={{0,2},{2,4},{4,6},{6,8},{8,10},{10,12},{12,14},{14,16},{16,18},{18... | collective-permute-start | bytes 1769480 | tf_op jit(solution)/shard_map/ppermute | solution.py:17
  15.3 17.0 %collective-permute-start.1 = (bf16[144,2048]{1,0:T(8,128)(2,1)S(1)}, bf16[144,2048]{1,0:T(8,128)(2,1)S(1)}, u32[]{:S(2)}, u32[]{:S(2)}) collective-permute-start(bf16[144,2048]{1,0:T(8,128)(2,1)S(1)} %get-tuple-element.14), channel_id=1, source_target_pairs={{2,0},{4,2},{6,4},{8,6},{10,8},{12,10},{14,12},{16,14},{18,16},{20... | collective-permute-start | bytes 1769480 | tf_op jit(solution)/shard_map/ppermute | solution.py:17
  16.7 49.9 %collective-permute-start.4 = (s32[144]{0:T(256)S(1)}, s32[144]{0:T(256)S(1)}, u32[]{:S(2)}, u32[]{:S(2)}) collective-permute-start(s32[144]{0:T(256)S(1)} %get-tuple-element.27), channel_id=1, source_target_pairs={{0,2},{2,4},{4,6},{6,8},{8,10},{10,12},{12,14},{14,16},{16,18},{18... | collective-permute-start | bytes 1736 | tf_op jit(solution)/shard_map/ppermute | solution.py:17
  21.8 44.7 %collective-permute-start.5 = (s32[144]{0:T(256)S(1)}, s32[144]{0:T(256)S(1)}, u32[]{:S(2)}, u32[]{:S(2)}) collective-permute-start(s32[144]{0:T(256)S(1)} %get-tuple-element.28), channel_id=1, source_target_pairs={{2,0},{4,2},{6,4},{8,6},{10,8},{12,10},{14,12},{16,14},{18,16},{20... | collective-permute-start | bytes 1736 | tf_op jit(solution)/shard_map/ppermute | solution.py:17
  24.0 43.9 %collective-permute-start.3 = (bf16[144,2048]{1,0:T(8,128)(2,1)}, bf16[144,2048]{1,0:T(8,128)(2,1)}, u32[]{:S(2)}, u32[]{:S(2)}) collective-permute-start(bf16[144,2048]{1,0:T(8,128)(2,1)} %slice.123), channel_id=1, source_target_pairs={{2,0},{4,2},{6,4},{8,6},{10,8},{12,10},{14,12},{16,14},{18,16},{20... | collective-permute-start | bytes 1769480 | tf_op jit(solution)/shard_map/ppermute | solution.py:17
  33.2 43.0 %collective-permute-start.2 = (bf16[544,2048]{1,0:T(8,128)(2,1)}, bf16[544,2048]{1,0:T(8,128)(2,1)}, u32[]{:S(2)}, u32[]{:S(2)}) collective-permute-start(bf16[544,2048]{1,0:T(8,128)(2,1)} %constant_dynamic-update-slice_fusion), channel_id=1, source_target_pairs={{0,1},{1,0},{2,3},{3,2},{4,5},{5,4},{6,7},{7,6},{8,9},{9,8},{10,11... | collective-permute-start | bytes 6684680 | tf_op jit(solution)/shard_map/ppermute | solution.py:22
  52.4 12.3 %copy-start.9 = (f32[3,128,7]{1,2,0:T(8,128)S(1)}, f32[3,128,7]{1,2,0:T(8,128)}, u32[]{:S(2)}) copy-start(f32[3,128,7]{1,2,0:T(8,128)} %param.8) | copy-start | bytes 32260
  69.0 6.1 %copy-start.2 = (bf16[400,2048]{1,0:T(8,128)(2,1)}, bf16[400,2048]{1,0:T(8,128)(2,1)S(1)}, u32[]{:S(2)}) copy-start(bf16[400,2048]{1,0:T(8,128)(2,1)S(1)} %constant_dynamic-update-slice_fusion.3.grad) | copy-start | bytes 4915204
  330.9 16.7 %slice-start = ((s8[9437184]{0:T(1024)(128)(4,1)}), s8[4194304]{0:T(1024)(128)(4,1)S(1)}, s32[]{:S(2)}) async-start(s8[9437184]{0:T(1024)(128)(4,1)} %bitcast.58), calls=%async_computation.2 | async-start | bytes 8388608
  330.9 16.7 %slice-start.1 = ((s8[9437184]{0:T(1024)(128)(4,1)}), s8[1048576]{0:T(1024)(128)(4,1)S(1)}, s32[]{:S(2)}) async-start(s8[9437184]{0:T(1024)(128)(4,1)} %bitcast.58), calls=%async_computation.3 | async-start | bytes 2097152
  338.4 9.3 %slice-start.2 = ((s8[9437184]{0:T(1024)(128)(4,1)}), s8[4194304]{0:T(1024)(128)(4,1)S(1)}, s32[]{:S(2)}) async-start(s8[9437184]{0:T(1024)(128)(4,1)} %bitcast.58), calls=%async_computation.4 | async-start | bytes 8388608
  338.4 9.3 %copy-start.4 = (f32[256,4096]{1,0:T(8,128)S(1)}, f32[256,4096]{1,0:T(8,128)}, u32[]{:S(2)}) copy-start(f32[256,4096]{1,0:T(8,128)} %convolution_bitcast_fusion) | copy-start | bytes 12582916
  338.4 9.3 %copy-start.6 = (bf16[3,256,384]{2,1,0:T(8,128)(2,1)S(1)}, bf16[3,256,384]{2,1,0:T(8,128)(2,1)}, u32[]{:S(2)}) copy-start(bf16[3,256,384]{2,1,0:T(8,128)(2,1)} %get-tuple-element.13) | copy-start | bytes 1769476
  346.1 5.4 %copy-start.7 = (bf16[256,1664]{1,0:T(8,128)(2,1)S(1)}, bf16[256,1664]{1,0:T(8,128)(2,1)}, u32[]{:S(2)}) copy-start(bf16[256,1664]{1,0:T(8,128)(2,1)} %get-tuple-element.8) | copy-start | bytes 2555908
  346.1 5.4 %copy-start.8 = (bf16[256,384]{1,0:T(8,128)(2,1)S(1)}, bf16[256,384]{1,0:T(8,128)(2,1)}, u32[]{:S(2)}) copy-start(bf16[256,384]{1,0:T(8,128)(2,1)} %get-tuple-element.11) | copy-start | bytes 589828
  346.1 14.8 %collective-permute-start.6 = (bf16[128,2048]{1,0:T(8,128)(2,1)S(1)}, bf16[128,2048]{1,0:T(8,128)(2,1)S(1)}, u32[]{:S(2)}, u32[]{:S(2)}) collective-permute-start(bf16[128,2048]{1,0:T(8,128)(2,1)S(1)} %constant_dynamic-slice_fusion.1), channel_id=1, source_target_pairs={{0,1},{1,0},{2,3},{3,2},{4,5},{5,4},{6,7},{7,6},{8,9},{9,8},{10,11... | collective-permute-start | bytes 1572872 | tf_op jit(solution)/shard_map/ppermute | solution.py:22
  347.7 25.0 %copy-start.1 = (bf16[128,128]{1,0:T(8,128)(2,1)S(1)}, bf16[128,128]{1,0:T(8,128)(2,1)}, u32[]{:S(2)}) copy-start(bf16[128,128]{1,0:T(8,128)(2,1)} %param.9) | copy-start | bytes 98308
  350.9 20.6 %collective-permute-start.7 = (bf16[128,2048]{1,0:T(8,128)(2,1)S(1)}, bf16[128,2048]{1,0:T(8,128)(2,1)S(1)}, u32[]{:S(2)}, u32[]{:S(2)}) collective-permute-start(bf16[128,2048]{1,0:T(8,128)(2,1)S(1)} %constant_dynamic-slice_fusion), channel_id=1, source_target_pairs={{0,1},{1,0},{2,3},{3,2},{4,5},{5,4},{6,7},{7,6},{8,9},{9,8},{10,11... | collective-permute-start | bytes 1572872 | tf_op jit(solution)/shard_map/ppermute | solution.py:22
Sparse Core Ops, SparseCore 0:
  10.8 218.2 all-gather.2
  232.0 85.8 all-gather.4
